TPU v7x, 32 devices: a whole 2x2x4 slice. The times are simulated.
32 devices in a mesh: wave: 8 (over z, x), parity: 2 (over y), lev: 2 (over core).
Axes of the slice: x: 2, y: 2, z: 4, core: 2. Of those that a mesh axis runs over, the one named last changes fastest.
Arguments:
- fourier: bfloat16 [2, 1280, 16, 256], P('parity', 'wave', None, 'lev'), may hold values from -6 to 6
- legendre: bfloat16 [16, 2, 1280, 1280], P('wave', 'parity', 'lev'), may hold values from -0.15625 to 0.15625
- quad_weights: float32 [1280], P('wave'), may hold values from 0.3 to 3
- slot_wave: int32 [16], replicated, may hold values from 0 to 15, as said below
- to_modes: float32 [128, 128], replicated, may hold values from -0.5 to 0.5
- from_modes: float32 [128, 128], replicated, may hold values from -0.5 to 0.5
- mode_rates: float32 [128], replicated, may hold values from 0.1 to 10
Outputs:
- columns: bfloat16 [2, 1280, 16, 256], P('parity', 'wave', None, 'lev')
- spectral: bfloat16 [2, 1280, 4096], P('parity', 'lev', 'wave')
Inputs may be any that keep to these rules, and one draw needn't show every extreme that they name: `slot_wave`: A permutation of the wavenumbers 0 to 15; the owner with index w on wave holds slots w * 2 to (w + 1) * 2 - 1. Slots 2 i and 2 i + 1 hold a wavenumber below 8 and 15 minus it, in that order.
All inputs are finite; a program needn't handle non-finite values.
Results may differ from a plain program's by a relative error of at most 0.014.
Values may be sent and summed in bfloat16 or wider, within the bound.
No kernel may reach another device: no remote copies, remote signals or barrier semaphores. Data moves between devices by JAX's collectives and lax.ppermute only.
A program may use at most 128 MiB of HBM per device.

v0:
```python
import jax
import jax.numpy as jnp
from jax import lax
from jax.sharding import PartitionSpec as P


def partner_2(value, axis, distance):
    mask = 2**distance
    pairs = [(source, source ^ mask) for source in range(lax.axis_size(axis))]
    return lax.ppermute(value, axis, pairs)


def combine(mine_part, partner, signed_one):
    return (partner.astype(jnp.float32) + signed_one * mine_part.astype(jnp.float32)).astype(
        jnp.bfloat16
    )


def widen_matrix(square):
    levels = square.shape[0]
    pair_eye = jnp.eye(2, dtype=jnp.float32)
    return (square[:, None, :, None] * pair_eye[None, :, None, :]).reshape(2 * levels, 2 * levels)


def per_device(fourier, legendre, quad_weights, slot_wave, to_modes, from_modes, mode_rates):
    parity = lax.axis_index("parity")
    signed_one = (1 - 2 * parity).astype(jnp.float32)
    levels = to_modes.shape[0]
    col_width = 2 * levels
    wave_count = slot_wave.shape[0]
    per_owner = legendre.shape[0]
    degrees = legendre.shape[3]
    top_degree = 2 * degrees - 1
    grid_block = fourier[0]
    scaled = (quad_weights[:, None, None] * grid_block.astype(jnp.float32)).astype(jnp.bfloat16)
    scaled = combine(scaled, partner_2(scaled, "parity", 0), signed_one)
    by_slot = jnp.transpose(jnp.take(scaled, slot_wave, axis=1), (1, 0, 2))
    arrived = lax.all_to_all(
        lax.all_to_all(by_slot, "wave", split_axis=0, concat_axis=1, tiled=True),
        "lev",
        split_axis=1,
        concat_axis=2,
        tiled=True,
    )
    owned_waves = lax.dynamic_slice_in_dim(slot_wave, lax.axis_index("wave") * per_owner, per_owner)
    to_wide = widen_matrix(jnp.transpose(to_modes))
    from_wide = widen_matrix(jnp.transpose(from_modes))
    rates_wide = jnp.repeat(mode_rates, 2)
    half_deg = degrees // lax.axis_size("lev")
    pieces = []
    for owned in range(per_owner):
        deg_block = legendre[owned, 0]
        pieces.append(
            lax.dot_general(
                deg_block,
                arrived[owned],
                (((0,), (0,)), ((), ())),
                preferred_element_type=jnp.float32,
            )
        )
    summed = lax.psum(jnp.concatenate(pieces, axis=1), "lev")
    row_count = summed.shape[0]
    degree_idx = jnp.arange(row_count, dtype=jnp.int32)
    degree = (owned_waves[None, :] + 2 * degree_idx[:, None] + parity).reshape(-1, 1)
    flat = summed.reshape(-1, col_width)
    kept = jnp.where(degree <= top_degree, flat, jnp.zeros_like(flat))
    degree_f = degree.astype(jnp.float32)
    stiffness = degree_f * (degree_f + 1.0) / (top_degree * (top_degree + 1.0))
    mode_part = jnp.dot(
        kept, to_wide, precision=lax.Precision.HIGHEST, preferred_element_type=jnp.float32
    )
    mode_part = mode_part / (1.0 + stiffness * rates_wide[None, :])
    updated = jnp.dot(
        mode_part, from_wide, precision=lax.Precision.HIGHEST, preferred_element_type=jnp.float32
    )
    updated = updated.reshape(row_count, per_owner * col_width).astype(jnp.bfloat16)
    sums = []
    for owned in range(per_owner):
        deg_block = legendre[owned, 0]
        coeffs = updated[:, owned * col_width : (owned + 1) * col_width]
        sums.append(jnp.dot(deg_block, coeffs, preferred_element_type=jnp.float32))
    grid_sums = jnp.stack(sums)
    spectral_mine = lax.dynamic_slice_in_dim(updated, lax.axis_index("lev") * half_deg, half_deg, 0)
    parts = grid_sums.astype(jnp.bfloat16)
    returned = lax.all_to_all(
        lax.all_to_all(parts, "lev", split_axis=2, concat_axis=1, tiled=True),
        "wave",
        split_axis=1,
        concat_axis=0,
        tiled=True,
    )
    returned = combine(returned, partner_2(returned, "parity", 0), signed_one)
    inverse_slot = (
        jnp.zeros((wave_count,), jnp.int32)
        .at[slot_wave]
        .set(jnp.arange(wave_count, dtype=jnp.int32))
    )
    columns = jnp.transpose(jnp.take(returned, inverse_slot, axis=0), (1, 0, 2))
    return (columns[None], spectral_mine[None])


def solution(mesh):
    in_specs = (
        P("parity", "wave", None, "lev"),
        P("wave", "parity", "lev", None),
        P("wave"),
        P(),
        P(),
        P(),
        P(),
    )
    out_specs = (P("parity", "wave", None, "lev"), P("parity", "lev", "wave"))
    return jax.shard_map(
        per_device, mesh=mesh, in_specs=in_specs, out_specs=out_specs, check_vma=False
    )
```

profile of v0, /device:TPU:0, one launch (start us, length us, event | category | flops | bytes accessed | tf_op | source)
XLA Modules:
  0.0 182.7 jit_solution(7377061069278927496)
XLA Ops:
  8.5 3.0 %collective-permute-start = (bf16[160,16,128]{2,0,1:T(8,128)(2,1)S(1)}, bf16[160,16,128]{2,0,1:T(8,128)(2,1)S(1)}, u32[]{:S(2)}, u32[]{:S(2)}) collective-permute-start(bf16[160,16,128]{2,0,1:T(8,128)(2,1)S(1)} %fusion.10), channel_id=1, source_target_pairs={{0,2},{2,0},{1,3},{3,1},{4,6},{6,4},{5,7},{7,5},{8,10},{10,8},{9,1... | collective-permute-start | bytes 1966088 | tf_op jit(solution)/shard_map/ppermute | solution.py:10
  12.9 13.4 %collective-permute-done = bf16[160,16,128]{2,0,1:T(8,128)(2,1)S(1)} collective-permute-done((bf16[160,16,128]{2,0,1:T(8,128)(2,1)S(1)}, bf16[160,16,128]{2,0,1:T(8,128)(2,1)S(1)}, u32[]{:S(2)}, u32[]{:S(2)}) %collective-permute-start) | collective-permute-done | bytes 655392 | tf_op jit(solution)/shard_map/ppermute | solution.py:10
  29.3 6.0 %all-to-all-start = ((bf16[16,160,128]{2,1,0:T(8,128)(2,1)}), bf16[16,160,128]{2,1,0:T(8,128)(2,1)S(1)}, u32[]{:S(2)}, u32[]{:S(2)}) async-start(bf16[16,160,128]{2,1,0:T(8,128)(2,1)} %broadcast_select_fusion), calls=%async_computation | async-start | bytes 1310720 | tf_op jit(solution)/shard_map/all_to_all | solution.py:39
  35.7 16.1 %all-to-all-done = bf16[16,160,128]{2,1,0:T(8,128)(2,1)S(1)} async-done(((bf16[16,160,128]{2,1,0:T(8,128)(2,1)}), bf16[16,160,128]{2,1,0:T(8,128)(2,1)S(1)}, u32[]{:S(2)}, u32[]{:S(2)}) %all-to-all-start) | async-done | bytes 655392 | tf_op jit(solution)/shard_map/all_to_all | solution.py:39
  51.9 5.4 %copy.50 = bf16[2,1280,128]{2,0,1:T(2,128)(2,1)S(1)} copy(bf16[2,1280,128]{2,1,0:T(8,128)(2,1)S(1)} %bitcast.76) | data formatting | bytes 1310720 | tf_op jit(solution)/shard_map/all_to_all | solution.py:39
  57.3 4.5 %all_to_all.69 = bf16[2,1280,128]{2,0,1:T(2,128)(2,1)S(1)} all-to-all(bf16[2,1280,128]{2,0,1:T(2,128)(2,1)S(1)} %copy.50), channel_id=1, replica_groups=mesh['wave'=8,'parity'=2,'lev'=2] {'lev'}, dimensions={1} | all-to-all | bytes 1310720 | tf_op jit(solution)/shard_map/all_to_all | solution.py:38
  62.8 1.9 %copy.53 = bf16[1,640,2,128]{1,3,2,0:T(8,128)(2,1)} copy(bf16[1,640,2,128]{3,1,2,0:T(8,128)(2,1)} %get-tuple-element.11) | data formatting | bytes 655360 | tf_op jit(solution)/shard_map/slice | solution.py:56
  64.7 1.9 %copy.52 = bf16[1,640,2,128]{1,3,2,0:T(8,128)(2,1)} copy(bf16[1,640,2,128]{3,1,2,0:T(8,128)(2,1)} %get-tuple-element.10) | data formatting | bytes 655360 | tf_op jit(solution)/shard_map/slice | solution.py:56
  66.5 1.7 convolution_bitcast_fusion
  68.9 1.7 pad_maximum_fusion
  70.7 12.3 %broadcast_multiply_fusion = (f32[128,2,128,2]{3,2,1,0:T(8,128)}, f32[128,2,128,2]{3,2,1,0:T(8,128)}) fusion(f32[128,128]{1,0:T(8,128)S(1)} %copy.57, f32[2,2]{1,0:T(2,128)S(1)} %compare_convert_fusion, f32[128,128]{1,0:T(8,128)S(1)} %copy.55), kind=kLoop, calls=%fused_computation.3 | loop fusion | flops 131072 | bytes 655376 | tf_op jit(solution)/shard_map/mul | solution.py:22
  83.0 13.2 %mul.114 = f32[256,256]{1,0:T(8,128)S(1)} reshape(f32[128,2,128,2]{3,2,1,0:T(8,128)} %get-tuple-element.13) | data formatting | bytes 524288 | tf_op jit(solution)/shard_map/mul | solution.py:22
  97.1 12.7 %mul.122 = f32[256,256]{1,0:T(8,128)S(1)} reshape(f32[128,2,128,2]{3,2,1,0:T(8,128)} %get-tuple-element.12) | data formatting | bytes 524288 | tf_op jit(solution)/shard_map/mul | solution.py:22
  109.9 1.9 %bitcast_select_fusion = f32[1280,512]{0,1:T(8,128)S(1)} fusion(f32[1280,512]{0,1:T(8,128)} %all-reduce.2.cloned.1.call-done, pred[1280,2]{0,1:T(4,128)(4,1)S(1)} %fusion.27), kind=kLoop, calls=%fused_computation.10 | loop fusion | flops 655360 | bytes 5245440 | tf_op jit(solution)/shard_map/jit(_where)/select_n | solution.py:66
  111.8 2.1 %copy.54 = f32[1280,512]{1,0:T(8,128)} copy(f32[1280,512]{0,1:T(8,128)S(1)} %bitcast_select_fusion) | data formatting | bytes 5242880 | tf_op jit(solution)/shard_map/jit(_where)/select_n | solution.py:66
  113.9 2.6 %select_n.45 = f32[2560,256]{1,0:T(8,128)S(1)} reshape(f32[1280,512]{1,0:T(8,128)} %copy.54) | data formatting | bytes 5242880 | tf_op jit(solution)/shard_map/jit(_where)/select_n | solution.py:66
  116.5 2.3 %convolution_divide_fusion = f32[2560,256]{1,0:T(8,128)S(1)} fusion(f32[2560,256]{1,0:T(8,128)S(1)} %select_n.45, f32[256,256]{1,0:T(8,128)S(1)} %mul.114, f32[256]{0:T(256)S(1)} %mul.117, f32[2560]{0:T(1024)S(1)} %fusion.25), kind=kOutput, calls=%fused_computation.6 | convolution fusion | flops 2015232000 | bytes 5516288 | tf_op jit(solution)/shard_map/dot_general | solution.py:69
  118.9 2.2 %convolution_convert_fusion = bf16[2560,256]{1,0:T(8,128)(2,1)S(1)} fusion(f32[2560,256]{1,0:T(8,128)S(1)} %convolution_divide_fusion, f32[256,256]{1,0:T(8,128)S(1)} %mul.122), kind=kOutput, calls=%fused_computation.5 | convolution fusion | flops 2013921280 | bytes 4194304 | tf_op jit(solution)/shard_map/dot_general | solution.py:73
  121.8 2.3 %fusion.17 = bf16[1,640,256]{1,2,0:T(8,128)(2,1)S(1)} fusion(bf16[2,1,640,1280]{3,2,1,0:T(8,128)(2,1)} %param.8, bf16[1280,512]{1,0:T(8,128)(2,1)S(1)} %convert_element_type.69), kind=kOutput, calls=%fused_computation.27 | convolution fusion | flops 419594240 | bytes 2621440 | tf_op jit(solution)/shard_map/dot_general | solution.py:81
  125.7 4.3 %all_to_all.70 = bf16[2,640,256]{1,0,2:T(2,128)(2,1)S(1)} all-to-all(bf16[2,640,256]{1,0,2:T(2,128)(2,1)S(1)} %copy.58), channel_id=1, replica_groups=mesh['wave'=8,'parity'=2,'lev'=2] {'lev'}, dimensions={2} | all-to-all | bytes 1310720 | tf_op jit(solution)/shard_map/all_to_all | solution.py:86
  130.4 6.2 %copy.61 = bf16[2,1280,128]{2,0,1:T(2,128)(2,1)} copy(bf16[2,1280,128]{2,1,0:T(8,128)(2,1)S(1)} %bitcast.78) | data formatting | bytes 1310720 | tf_op jit(solution)/shard_map/all_to_all | solution.py:86
  136.5 3.6 %all-to-all-start.3 = ((bf16[2,1280,128]{2,0,1:T(2,128)(2,1)}), bf16[2,1280,128]{2,0,1:T(2,128)(2,1)S(1)}, u32[]{:S(2)}, u32[]{:S(2)}) async-start(bf16[2,1280,128]{2,0,1:T(2,128)(2,1)} %copy.61), calls=%async_computation.3 | async-start | bytes 1310720 | tf_op jit(solution)/shard_map/all_to_all | solution.py:85
  140.7 17.1 %all-to-all-done.3 = bf16[2,1280,128]{2,0,1:T(2,128)(2,1)S(1)} async-done(((bf16[2,1280,128]{2,0,1:T(2,128)(2,1)}), bf16[2,1280,128]{2,0,1:T(2,128)(2,1)S(1)}, u32[]{:S(2)}, u32[]{:S(2)}) %all-to-all-start.3) | async-done | bytes 655392 | tf_op jit(solution)/shard_map/all_to_all | solution.py:85
  160.4 13.2 %collective-permute-done.1 = bf16[16,160,128]{2,1,0:T(8,128)(2,1)S(1)} collective-permute-done((bf16[16,160,128]{2,1,0:T(8,128)(2,1)S(1)}, bf16[16,160,128]{2,1,0:T(8,128)(2,1)S(1)}, u32[]{:S(2)}, u32[]{:S(2)}) %collective-permute-start.1) | collective-permute-done | bytes 655392 | tf_op jit(solution)/shard_map/ppermute | solution.py:10
  (59 shorter events, 16.7 us)
Async XLA Ops:
  8.5 17.8 %collective-permute-start = (bf16[160,16,128]{2,0,1:T(8,128)(2,1)S(1)}, bf16[160,16,128]{2,0,1:T(8,128)(2,1)S(1)}, u32[]{:S(2)}, u32[]{:S(2)}) collective-permute-start(bf16[160,16,128]{2,0,1:T(8,128)(2,1)S(1)} %fusion.10), channel_id=1, source_target_pairs={{0,2},{2,0},{1,3},{3,1},{4,6},{6,4},{5,7},{7,5},{8,10},{10,8},{9,1... | collective-permute-start | bytes 1966088 | tf_op jit(solution)/shard_map/ppermute | solution.py:10
  12.8 22.6 %copy-start.6 = (s32[16]{0:T(128)S(1)}, s32[16]{0:T(128)}, u32[]{:S(2)}) copy-start(s32[16]{0:T(128)} %param.10) | copy-start | bytes 196
  12.8 22.6 %copy-start.3 = (f32[128,128]{1,0:T(8,128)S(1)}, f32[128,128]{1,0:T(8,128)}, u32[]{:S(2)}) copy-start(f32[128,128]{1,0:T(8,128)} %param.12) | copy-start | bytes 196612
  12.8 22.7 %copy-start.4 = (f32[128,128]{1,0:T(8,128)S(1)}, f32[128,128]{1,0:T(8,128)}, u32[]{:S(2)}) copy-start(f32[128,128]{1,0:T(8,128)} %param.11) | copy-start | bytes 196612
  29.3 22.5 %all-to-all-start = ((bf16[16,160,128]{2,1,0:T(8,128)(2,1)}), bf16[16,160,128]{2,1,0:T(8,128)(2,1)S(1)}, u32[]{:S(2)}, u32[]{:S(2)}) async-start(bf16[16,160,128]{2,1,0:T(8,128)(2,1)} %broadcast_select_fusion), calls=%async_computation | async-start | bytes 1310720 | tf_op jit(solution)/shard_map/all_to_all | solution.py:39
  35.3 74.5 %all-reduce.2.cloned.1.call-start = ((), (), s32[]{:S(2)}) async-start(), calls=%async_computation.4 | async-start | bytes 5242880 | tf_op jit(solution)/shard_map/psum | solution.py:61
  57.3 9.2 %copy-start = (bf16[2,1,640,1280]{3,2,1,0:T(8,128)(2,1)S(1)}, bf16[2,1,640,1280]{3,2,1,0:T(8,128)(2,1)}, u32[]{:S(2)}) copy-start(bf16[2,1,640,1280]{3,2,1,0:T(8,128)(2,1)} %param.8) | copy-start | bytes 9830404
  66.5 1.7 copy-start.2
  83.0 13.2 %copy-start.5 = (f32[128]{0:T(128)S(1)}, f32[128]{0:T(128)}, u32[]{:S(2)}) copy-start(f32[128]{0:T(128)} %param.13) | copy-start | bytes 1540
  121.8 2.4 %copy-start.1 = (bf16[2,1,640,1280]{3,2,1,0:T(8,128)(2,1)S(1)}, bf16[2,1,640,1280]{3,2,1,0:T(8,128)(2,1)}, u32[]{:S(2)}) copy-start(bf16[2,1,640,1280]{3,2,1,0:T(8,128)(2,1)} %param.8) | copy-start | bytes 9830404
  136.5 21.3 %all-to-all-start.3 = ((bf16[2,1280,128]{2,0,1:T(2,128)(2,1)}), bf16[2,1280,128]{2,0,1:T(2,128)(2,1)S(1)}, u32[]{:S(2)}, u32[]{:S(2)}) async-start(bf16[2,1280,128]{2,0,1:T(2,128)(2,1)} %copy.61), calls=%async_computation.3 | async-start | bytes 1310720 | tf_op jit(solution)/shard_map/all_to_all | solution.py:85
  158.0 15.6 %collective-permute-start.1 = (bf16[16,160,128]{2,1,0:T(8,128)(2,1)S(1)}, bf16[16,160,128]{2,1,0:T(8,128)(2,1)S(1)}, u32[]{:S(2)}, u32[]{:S(2)}) collective-permute-start(bf16[16,160,128]{2,1,0:T(8,128)(2,1)S(1)} %bitcast.74), channel_id=1, source_target_pairs={{0,2},{2,0},{1,3},{3,1},{4,6},{6,4},{5,7},{7,5},{8,10},{10,8},{9,1... | collective-permute-start | bytes 1966088 | tf_op jit(solution)/shard_map/ppermute | solution.py:10
Sparse Core Ops, SparseCore 0:
  70.8 21.2 all-reduce.1
where the time goes:
time: 184 us; the launch traced here: 183 us
  waiting for transfers between devices  59.9 us (33%)
  local copies, waits for them, and re-layouts  53.9 us (29%)
  other arithmetic  21.6 us (12%)
  between operations  14.3 us (8%)
  starting transfers between devices  14.1 us (8%)
  matrix products  9.95 us (5%)
  blocking collectives  8.78 us (5%)
    ppermute x2, waiting for transfers between devices, partner_2(): return lax.ppermute(value, axis, pairs)  26.6 us
    mul x2, local copies, waits for them, and re-layouts, widen_matrix(): square[:, None, :, None] * pair_eye[None, :, None, :]  25.9 us
    all_to_all x1, waiting for transfers between devices, per_device(): lax.all_to_all(lax.all_to_all(parts, 'lev', split_axis=2, concat_axis=1,...  17.1 us
    all_to_all x1, waiting for transfers between devices, per_device(): lax.all_to_all(by_slot, 'wave', split_axis=0, concat_axis=1, tiled=True)  16.1 us
    mul x1, other arithmetic, widen_matrix(): square[:, None, :, None] * pair_eye[None, :, None, :]  12.3 us
    all_to_all x3, local copies, waits for them, and re-layouts, per_device(): lax.all_to_all(parts, 'lev', split_axis=2, concat_axis=1, tiled=True)  6.55 us
    all_to_all x1, starting transfers between devices, per_device(): lax.all_to_all(by_slot, 'wave', split_axis=0, concat_axis=1, tiled=True)  6.03 us
    all_to_all x2, local copies, waits for them, and re-layouts, per_device(): lax.all_to_all(by_slot, 'wave', split_axis=0, concat_axis=1, tiled=True)  5.49 us
  transfers between devices with their start and end apart: 5, of which 4 were waited for; matrix products, arithmetic and copies ran while one was open for 23% of the time, Pallas kernels for 0%

commit v1 on v0

--- a/solution.py
+++ b/solution.py
@@ -1,7 +1,16 @@
+import functools
+
 import jax
 import jax.numpy as jnp
 from jax import lax
+from jax.experimental import pallas as pl
+from jax.experimental.pallas import tpu as pltpu
 from jax.sharding import PartitionSpec as P
+
+AXES = ("wave", "parity", "lev")
+VMEM = pl.BlockSpec(memory_space=pltpu.VMEM)
+SMEM = pl.BlockSpec(memory_space=pltpu.SMEM)
+MIB = 1024 * 1024
 
 
 def partner_2(value, axis, distance):
@@ -16,13 +25,311 @@
     )
 
 
+def mask_plan(owners):
+    ring = owners // 2
+
+    def hops(mask):
+        step = mask >> 1
+        return min(step, ring - step) + (mask & 1)
+
+    plan = []
+    for core in range(2):
+        masks = [m for m in range(owners) if (m >> 1) & 1 == core]
+        masks.sort(key=lambda m: (hops(m), m))
+        half = len(masks) // 2
+        plan.append((masks[:half], masks[half:]))
+    return plan
+
+
+def meet(value, masks):
+    owners, hemis = lax.axis_size("wave"), lax.axis_size("parity")
+    pairs = []
+    for wave in range(owners):
+        for hemi in range(hemis):
+            for core, mask in enumerate(masks):
+                if mask:
+                    source = (wave * hemis + hemi) * 2 + core
+                    target = ((wave ^ mask) * hemis + hemi) * 2 + core
+                    pairs.append((source, target))
+    return lax.ppermute(value, AXES, pairs)
+
+
+def near_exchange(blocks, plan, lev):
+    arrived = []
+    for i, block in enumerate(blocks):
+        masks = (plan[0][0][i], plan[1][0][i])
+        got = meet(block, masks)
+        if not masks[0]:
+            got = jnp.where(lev == 0, block, got)
+        arrived.append(got)
+    keep = jnp.stack([a[0] for a in arrived])
+    give = jnp.stack([a[1] for a in arrived])
+    got = partner_2(give, "lev", 0)
+    return keep, partner_2(keep, "parity", 0), got, partner_2(got, "parity", 0)
+
+
+def far_exchange(blocks, plan):
+    arrived = [
+        meet(block, (plan[0][1][i], plan[1][1][i])) for i, block in enumerate(blocks)
+    ]
+    give = jnp.stack([a[1] for a in arrived])
+    return arrived, partner_2(give, "lev", 0)
+
+
+def scale_kernel(meta, slots, mine, other, weights, near, far, held):
+    rows, waves, width = mine.shape
+    lev = meta[0]
+    held[0] = mine[...].astype(jnp.float32).reshape(rows * waves, width)
+    held[1] = other[...].astype(jnp.float32).reshape(rows * waves, width)
+    scale = weights[...]
+    count = near.shape[0]
+    for out, base in ((near, 1), (far, 1 + count)):
+        for i in range(count):
+            owner = meta[base + i]
+            for part in range(2):
+                slot = 2 * owner + (lev if part == 0 else 1 - lev)
+                wave = slots[slot]
+                for source in range(2):
+                    picked = held[source, pl.ds(wave, rows, stride=waves), :]
+                    place = (lev if source == 0 else 1 - lev) * width
+                    out[i, part, :, pl.ds(pl.multiple_of(place, width), width)] = (
+                        scale * picked
+                    ).astype(jnp.bfloat16)
+
+
+def solve_kernel(
+    meta,
+    keep,
+    keep_peer,
+    got,
+    got_peer,
+    *refs,
+    count,
+):
+    far = refs[:count]
+    far_got, table_mine, table_other, to_modes, from_modes, rates = refs[count : count + 6]
+    (spec_mine, spec_other, near_mine, near_other, far_mine, far_other, data, spec, parts) = refs[
+        count + 6 :
+    ]
+    lev, parity, wavenum = meta[0], meta[1], meta[2]
+    rows = keep.shape[1]
+    half, degrees = table_mine.shape
+    width = data.shape[1]
+    sign = (1 - 2 * parity).astype(jnp.float32)
+
+    def place(index):
+        return pl.ds(pl.multiple_of(meta[3 + index] * rows, 16), rows)
+
+    def fold(own, peer):
+        return (peer.astype(jnp.float32) + sign * own.astype(jnp.float32)).astype(jnp.bfloat16)
+
+    for i in range(count):
+        data[place(i), :] = fold(keep[i], keep_peer[i])
+        data[place(count + i), :] = fold(got[i], got_peer[i])
+        data[place(2 * count + i), :] = far[i][0]
+        data[place(3 * count + i), :] = far_got[i]
+    at_mine = pl.ds(pl.multiple_of(lev * half, 16), half)
+    at_other = pl.ds(pl.multiple_of((1 - lev) * half, 16), half)
+    rows_first = (((0,), (0,)), ((), ()))
+    raw = lax.dot_general(
+        data[at_mine, :], table_mine[...], rows_first, preferred_element_type=jnp.float32
+    ) + lax.dot_general(
+        data[at_other, :], table_other[...], rows_first, preferred_element_type=jnp.float32
+    )
+    top_degree = 2 * degrees - 1
+    degree = wavenum + parity + 2 * lax.broadcasted_iota(jnp.int32, (1, degrees), 1)
+    kept = jnp.where(degree <= top_degree, raw, 0.0)
+    degree_f = degree.astype(jnp.float32)
+    stiffness = degree_f * (degree_f + 1.0) / (top_degree * (top_degree + 1.0))
+
+    levels = to_modes.shape[0]
+    spread = (
+        (lax.broadcasted_iota(jnp.int32, (width, levels), 0) >> 1)
+        == lax.broadcasted_iota(jnp.int32, (width, levels), 1)
+    ).astype(jnp.float32)
+    same = (
+        (
+            lax.broadcasted_iota(jnp.int32, (width, width), 0)
+            + lax.broadcasted_iota(jnp.int32, (width, width), 1)
+        )
+        & 1
+    ) == 0
+    exact = functools.partial(
+        lax.dot_general,
+        precision=lax.Precision.HIGHEST,
+        preferred_element_type=jnp.float32,
+    )
+    plain = (((1,), (0,)), ((), ()))
+
+    def widen(square):
+        tall = exact(spread, square[...], plain)
+        return jnp.where(same, exact(tall, spread, (((1,), (1,)), ((), ()))), 0.0)
+
+    rate = jnp.sum(spread * rates[...], axis=1, keepdims=True)
+    modal = exact(widen(to_modes), kept, plain)
+    damped = modal / (1.0 + stiffness * rate)
+    updated = exact(widen(from_modes), damped, plain)
+    spec[...] = jnp.transpose(updated).astype(jnp.bfloat16)
+    part_mine = jnp.dot(table_mine[...], spec[...], preferred_element_type=jnp.float32)
+    parts[at_mine, :] = part_mine.astype(jnp.bfloat16)
+    part_other = jnp.dot(table_other[...], spec[...], preferred_element_type=jnp.float32)
+    parts[at_other, :] = part_other.astype(jnp.bfloat16)
+    spec_mine[...] = spec[at_mine, :]
+    spec_other[...] = spec[at_other, :]
+    side = width // 2
+    first = pl.ds(pl.multiple_of(lev * side, side), side)
+    second = pl.ds(pl.multiple_of((1 - lev) * side, side), side)
+    for out, base, order in (
+        (near_mine, 0, (first, second)),
+        (near_other, count, (second, first)),
+        (far_mine, 2 * count, (first, second)),
+        (far_other, 3 * count, (second, first)),
+    ):
+        for i in range(count):
+            for part in range(2):
+                out[i, part] = parts[place(base + i), order[part]]
+
+
+def place_kernel(meta, slots, keep, keep_peer, got, got_peer, *refs, count):
+    far = refs[:count]
+    far_got, out, held = refs[count:]
+    lev, parity = meta[0], meta[1]
+    rows, waves, width = out.shape
+    sign = (1 - 2 * parity).astype(jnp.float32)
+
+    def fold(own, peer):
+        return (peer.astype(jnp.float32) + sign * own.astype(jnp.float32)).astype(jnp.bfloat16)
+
+    for i in range(count):
+        for part in range(2):
+            mine = lev if part == 0 else 1 - lev
+            other = 1 - mine
+            for index, core, value in (
+                (i, mine, fold(keep[i, part], keep_peer[i, part])),
+                (count + i, other, fold(got[i, part], got_peer[i, part])),
+                (2 * count + i, mine, far[i][0, part]),
+                (3 * count + i, other, far_got[i, part]),
+            ):
+                wave = slots[2 * meta[3 + index] + core]
+                held[pl.ds(wave, rows, stride=waves), :] = value.astype(jnp.float32)
+    out[...] = held[...].reshape(rows, waves, width).astype(jnp.bfloat16)
+
+
+def params(mebibytes):
+    return pltpu.CompilerParams(vmem_limit_bytes=mebibytes * MIB)
+
+
+def per_device(fourier, legendre, quad_weights, slot_wave, to_modes, from_modes, mode_rates):
+    wave = lax.axis_index("wave").astype(jnp.int32)
+    parity = lax.axis_index("parity").astype(jnp.int32)
+    lev = lax.axis_index("lev").astype(jnp.int32)
+    signed_one = (1 - 2 * parity).astype(jnp.float32)
+    owners = lax.axis_size("wave")
+    plan = mask_plan(owners)
+    count = owners // 4
+    rows, waves, side = fourier.shape[1:]
+    width = 2 * side
+    half, degrees = legendre.shape[2:]
+    bf16 = jnp.bfloat16
+
+    def masks(core, kind):
+        return jnp.asarray(plan[core][kind], jnp.int32)
+
+    def owners_met(kind, sibling):
+        first, second = masks(0, kind), masks(1, kind)
+        return wave ^ jnp.where((lev == 0) != sibling, first, second)
+
+    near_ids, near_ids_other = owners_met(0, False), owners_met(0, True)
+    far_ids, far_ids_other = owners_met(1, False), owners_met(1, True)
+
+    grid_mine = fourier[0]
+    grid_other = partner_2(grid_mine, "lev", 0)
+    block = jax.ShapeDtypeStruct((count, 2, rows, width), bf16)
+    near, far = pl.pallas_call(
+        scale_kernel,
+        out_shape=(block, block),
+        in_specs=[SMEM, SMEM, VMEM, VMEM, VMEM],
+        out_specs=(VMEM, VMEM),
+        scratch_shapes=[pltpu.VMEM((2, rows * waves, side), jnp.float32)],
+        compiler_params=params(16),
+        name="scale",
+    )(
+        jnp.concatenate([lev[None], near_ids, far_ids]),
+        slot_wave,
+        grid_mine,
+        grid_other,
+        quad_weights[:, None],
+    )
+    far_folded = combine(far, partner_2(far, "parity", 0), signed_one)
+    near_parts = near_exchange([near[i] for i in range(count)], plan, lev)
+    far_arrived, far_got = far_exchange([far_folded[i] for i in range(count)], plan)
+
+    table_mine = lax.dynamic_index_in_dim(legendre[:, 0], lev, 0, False)
+    table_other = partner_2(lax.dynamic_index_in_dim(legendre[:, 0], 1 - lev, 0, False), "lev", 0)
+    wavenum = lax.dynamic_slice_in_dim(slot_wave, 2 * wave + lev, 1)
+    meta = jnp.concatenate(
+        [lev[None], parity[None], wavenum, near_ids, near_ids_other, far_ids, far_ids_other]
+    )
+    spec_shape = jax.ShapeDtypeStruct((half, width), bf16)
+    piece = jax.ShapeDtypeStruct((count, 2, rows, side), bf16)
+    outs = pl.pallas_call(
+        functools.partial(solve_kernel, count=count),
+        out_shape=(spec_shape, spec_shape, piece, piece, piece, piece),
+        in_specs=[SMEM] + [VMEM] * (10 + count),
+        out_specs=(VMEM,) * 6,
+        scratch_shapes=[pltpu.VMEM((2 * half, width), bf16)] * 3,
+        compiler_params=params(32),
+        name="solve",
+    )(
+        meta,
+        *near_parts,
+        *far_arrived,
+        far_got,
+        table_mine,
+        table_other,
+        to_modes,
+        from_modes,
+        mode_rates[None, :],
+    )
+    spec_mine, spec_other, near_mine, near_other, far_mine, far_other = outs
+    spec_got = partner_2(spec_other, "lev", 0)
+    spectral = jnp.where(
+        lev == 0,
+        jnp.concatenate([spec_mine, spec_got], axis=1),
+        jnp.concatenate([spec_got, spec_mine], axis=1),
+    )
+
+    far_from_other = partner_2(far_other, "lev", 0)
+    near_from_other = partner_2(near_other, "lev", 0)
+    far_folded = jnp.stack(
+        [
+            combine(far_mine, partner_2(far_mine, "parity", 0), signed_one),
+            combine(far_from_other, partner_2(far_from_other, "parity", 0), signed_one),
+        ],
+        axis=2,
+    )
+    near = jnp.stack([near_mine, near_from_other], axis=2)
+    near_parts = near_exchange([near[i] for i in range(count)], plan, lev)
+    far_arrived, far_got = far_exchange([far_folded[i] for i in range(count)], plan)
+    columns = pl.pallas_call(
+        functools.partial(place_kernel, count=count),
+        out_shape=jax.ShapeDtypeStruct((rows, waves, side), bf16),
+        in_specs=[SMEM, SMEM] + [VMEM] * (5 + count),
+        out_specs=VMEM,
+        scratch_shapes=[pltpu.VMEM((rows * waves, side), jnp.float32)],
+        compiler_params=params(16),
+        name="place",
+    )(meta, slot_wave, *near_parts, *far_arrived, far_got)
+    return (columns[None], spectral[None])
+
+
 def widen_matrix(square):
     levels = square.shape[0]
     pair_eye = jnp.eye(2, dtype=jnp.float32)
     return (square[:, None, :, None] * pair_eye[None, :, None, :]).reshape(2 * levels, 2 * levels)
 
 
-def per_device(fourier, legendre, quad_weights, slot_wave, to_modes, from_modes, mode_rates):
+def per_device_many(fourier, legendre, quad_weights, slot_wave, to_modes, from_modes, mode_rates):
     parity = lax.axis_index("parity")
     signed_one = (1 - 2 * parity).astype(jnp.float32)
     levels = to_modes.shape[0]
@@ -110,6 +417,11 @@
         P(),
     )
     out_specs = (P("parity", "wave", None, "lev"), P("parity", "lev", "wave"))
+    few = mesh.shape["wave"] in (4, 8, 16) and mesh.shape["lev"] == 2
     return jax.shard_map(
-        per_device, mesh=mesh, in_specs=in_specs, out_specs=out_specs, check_vma=False
-    )
+        per_device if few else per_device_many,
+        mesh=mesh,
+        in_specs=in_specs,
+        out_specs=out_specs,
+        check_vma=False,
+    )

time: 184 us -> 85 us (0.46)
  local copies, waits for them, and re-layouts: 53.9 us -> 12.1 us
  waiting for transfers between devices: 59.9 us -> 31.1 us
  other arithmetic: 21.6 us -> 3.79 us
  between operations: 14.3 us -> 0.91 us
  starting transfers between devices: 14.1 us -> 26 us
  Pallas kernels: 0 us -> 10.7 us
  matrix products: 9.95 us -> 0 us
  blocking collectives: 8.78 us -> 0 us
    all_to_all x2 -> x0, waiting for transfers between devices: 33.3 us -> none  [the longest x1 17.1 us: per_device(): lax.all_to_all(lax.all_to_all(parts, 'lev', split_axis=2, concat_axis=1,...]
    mul x3 -> x0, local copies, waits for them, and re-layouts: 26 us -> none  [the longest x2 25.9 us: widen_matrix(): square[:, None, :, None] * pair_eye[None, :, None, :]]
    ppermute x0 -> x8, waiting for transfers between devices: none -> 16.6 us  [meet(): return lax.ppermute(value, AXES, pairs)]
    mul x2 -> x0, other arithmetic: 12.3 us -> none  [the longest x1 12.3 us: widen_matrix(): square[:, None, :, None] * pair_eye[None, :, None, :]]
    all_to_all x8 -> x0, local copies, waits for them, and re-layouts: 12.3 us -> none  [the longest x3 6.55 us: per_device(): lax.all_to_all(parts, 'lev', split_axis=2, concat_axis=1, tiled=True)]
    ppermute x2 -> x16, waiting for transfers between devices: 26.6 us -> 14.4 us  [partner_2(): return lax.ppermute(value, axis, pairs)]
    ppermute x0 -> x8, starting transfers between devices: none -> 11 us  [meet(): return lax.ppermute(value, AXES, pairs)]
    pallas_call x0 -> x3, Pallas kernels: none -> 10.7 us  [the longest x1 7.09 us: per_device(): pl.pallas_call(functools.partial(solve_kernel, count=count), out_shape=(s...]
  transfers between devices with their start and end apart: 5 -> 24, of which waited for: 4 -> 10; matrix products, arithmetic and copies ran while one was open for 23% -> 11% of each run, Pallas kernels for 0% -> 0%
where the time goes in v1:
time: 85 us; the launch traced here: 84.6 us
  waiting for transfers between devices  31.1 us (37%)
  starting transfers between devices  26 us (31%)
  local copies, waits for them, and re-layouts  12.1 us (14%)
  Pallas kernels  10.7 us (13%)
  other arithmetic  3.79 us (4%)
  between operations  0.91 us (1%)
    ppermute x8, waiting for transfers between devices, meet(): return lax.ppermute(value, AXES, pairs)  16.6 us
    ppermute x16, starting transfers between devices, partner_2(): return lax.ppermute(value, axis, pairs)  15.1 us
    ppermute x16, waiting for transfers between devices, partner_2(): return lax.ppermute(value, axis, pairs)  14.4 us
    ppermute x8, starting transfers between devices, meet(): return lax.ppermute(value, AXES, pairs)  11 us
    pallas_call x1, Pallas kernels, per_device(): pl.pallas_call(functools.partial(solve_kernel, count=count), out_shape=(s...  7.09 us
    unnamed x26, local copies, waits for them, and re-layouts  5.85 us
    squeeze x1, local copies, waits for them, and re-layouts, per_device(): lax.dynamic_index_in_dim(legendre[:, 0], 1 - lev, 0, False)  3.33 us
    pallas_call x1, Pallas kernels, per_device(): pl.pallas_call(functools.partial(place_kernel, count=count), out_shape=ja...  2.19 us
  transfers between devices with their start and end apart: 24, of which 10 were waited for; matrix products, arithmetic and copies ran while one was open for 11% of the time, Pallas kernels for 0%

profile of v1, /device:TPU:0, one launch (start us, length us, event | category | flops | bytes accessed | tf_op | source)
XLA Modules:
  0.0 84.6 jit_solution(1785813105944559426)
XLA Ops:
  3.1 1.1 %copy-done.1 = bf16[1,160,16,128]{3,2,1,0:T(8,128)(2,1)S(1)} copy-done((bf16[1,160,16,128]{3,2,1,0:T(8,128)(2,1)S(1)}, bf16[1,160,16,128]{3,2,1,0:T(8,128)(2,1)}, u32[]{:S(2)}) %copy-start.1) | copy-done | bytes 655384
  4.8 1.4 %scale.1 = (bf16[2,2,160,256]{3,2,1,0:T(8,128)(2,1)S(1)}, bf16[2,2,160,256]{3,2,1,0:T(8,128)(2,1)S(1)}) custom-call(s32[5]{0:T(128)S(1)} %pad_add_fusion.meta, s32[16]{0:T(128)S(1)} %copy-done.10, bf16[160,16,128]{2,1,0:T(8,128)(2,1)S(1)} %bitcast.39, bf16[160,16,128]{2,1,0:T(8,128)(2,1)S(1)} %collective-permute-done.other, f32[160,1]{1,0:T(8,128)S(1)} %copy.18.weights), custom_call_target="tpu_custom_call" | custom-call | tf_op jit(solution)/shard_map/scale/pallas_call | solution.py:248
  7.1 1.3 %collective-permute-start.1 = (bf16[2,160,256]{2,1,0:T(8,128)(2,1)S(1)}, bf16[2,160,256]{2,1,0:T(8,128)(2,1)}, u32[]{:S(2)}, u32[]{:S(2)}) collective-permute-start(bf16[2,160,256]{2,1,0:T(8,128)(2,1)S(1)} %get-tuple-element.26), channel_id=1, source_target_pairs={{1,9},{3,11},{5,13},{7,15},{9,1},{11,3},{13,5},{15,7},{17,25},{19,... | collective-permute-start | bytes 491528 | tf_op jit(solution)/shard_map/ppermute | solution.py:54
  8.4 3.3 %dynamic-slice_bitcast_fusion = (bf16[640,1280]{1,0:T(8,128)(2,1)}, bf16[640,1280]{1,0:T(8,128)(2,1)S(1)}) fusion(bf16[2,1,640,1280]{3,2,1,0:T(8,128)(2,1)} %param.16, s32[]{:T(128)S(6)} %select_n.74, s32[]{:T(128)S(6)} %select_n.73), kind=kLoop, calls=%fused_computation | loop fusion | bytes 6553608 | tf_op jit(solution)/shard_map/jit(dynamic_index_in_dim)/squeeze | solution.py:268
  11.8 3.4 %collective-permute-start.10 = (bf16[640,1280]{1,0:T(8,128)(2,1)}, bf16[640,1280]{1,0:T(8,128)(2,1)S(1)}, u32[]{:S(2)}, u32[]{:S(2)}) collective-permute-start(bf16[640,1280]{1,0:T(8,128)(2,1)} %get-tuple-element.18), channel_id=1, source_target_pairs={{0,1},{1,0},{2,3},{3,2},{4,5},{5,4},{6,7},{7,6},{8,9},{9,8},{10,11... | collective-permute-start | bytes 4915208 | tf_op jit(solution)/shard_map/ppermute | solution.py:19
  15.2 1.5 %collective-permute-start.2 = (bf16[2,160,256]{2,1,0:T(8,128)(2,1)}, bf16[2,160,256]{2,1,0:T(8,128)(2,1)S(1)}, u32[]{:S(2)}, u32[]{:S(2)}) collective-permute-start(bf16[2,160,256]{2,1,0:T(8,128)(2,1)} %get-tuple-element.27), channel_id=1, source_target_pairs={{0,4},{1,25},{2,6},{3,27},{4,0},{5,29},{6,2},{7,31},{8,12},{9,17},... | collective-permute-start | bytes 491528 | tf_op jit(solution)/shard_map/ppermute | solution.py:54
  16.6 1.5 %collective-permute-start.6 = (bf16[2,2,160,256]{3,2,1,0:T(8,128)(2,1)}, bf16[2,2,160,256]{3,2,1,0:T(8,128)(2,1)S(1)}, u32[]{:S(2)}, u32[]{:S(2)}) collective-permute-start(bf16[2,2,160,256]{3,2,1,0:T(8,128)(2,1)} %copy-done.6), channel_id=1, source_target_pairs={{0,2},{2,0},{1,3},{3,1},{4,6},{6,4},{5,7},{7,5},{8,10},{10,8},{9,1... | collective-permute-start | bytes 983048 | tf_op jit(solution)/shard_map/ppermute | solution.py:19
  19.2 1.5 %collective-permute-done.2 = bf16[2,160,256]{2,1,0:T(8,128)(2,1)S(1)} collective-permute-done((bf16[2,160,256]{2,1,0:T(8,128)(2,1)}, bf16[2,160,256]{2,1,0:T(8,128)(2,1)S(1)}, u32[]{:S(2)}, u32[]{:S(2)}) %collective-permute-start.2) | collective-permute-done | bytes 163872 | tf_op jit(solution)/shard_map/ppermute | solution.py:54
  21.6 5.6 %collective-permute-done.6 = bf16[2,2,160,256]{3,2,1,0:T(8,128)(2,1)S(1)} collective-permute-done((bf16[2,2,160,256]{3,2,1,0:T(8,128)(2,1)}, bf16[2,2,160,256]{3,2,1,0:T(8,128)(2,1)S(1)}, u32[]{:S(2)}, u32[]{:S(2)}) %collective-permute-start.6) | collective-permute-done | bytes 327712 | tf_op jit(solution)/shard_map/ppermute | solution.py:19
  27.3 1.5 %collective-permute-start.8 = (bf16[2,160,256]{2,1,0:T(8,128)(2,1)S(1)}, bf16[2,160,256]{2,1,0:T(8,128)(2,1)S(1)}, u32[]{:S(2)}, u32[]{:S(2)}) collective-permute-start(bf16[2,160,256]{2,1,0:T(8,128)(2,1)S(1)} %get-tuple-element.24), channel_id=1, source_target_pairs={{0,20},{1,29},{2,22},{3,31},{4,16},{5,25},{6,18},{7,27},{8,28},{9,... | collective-permute-start | bytes 491528 | tf_op jit(solution)/shard_map/ppermute | solution.py:54
  28.8 1.1 %collective-permute-start.7 = (bf16[2,160,256]{2,1,0:T(8,128)(2,1)S(1)}, bf16[2,160,256]{2,1,0:T(8,128)(2,1)S(1)}, u32[]{:S(2)}, u32[]{:S(2)}) collective-permute-start(bf16[2,160,256]{2,1,0:T(8,128)(2,1)S(1)} %get-tuple-element.25), channel_id=1, source_target_pairs={{0,16},{1,13},{2,18},{3,15},{4,20},{5,9},{6,22},{7,11},{8,24},{9,5... | collective-permute-start | bytes 491528 | tf_op jit(solution)/shard_map/ppermute | solution.py:54
  29.9 1.6 %collective-permute-start.3 = (bf16[2,160,256]{2,1,0:T(8,128)(2,1)S(1)}, bf16[2,160,256]{2,1,0:T(8,128)(2,1)}, u32[]{:S(2)}, u32[]{:S(2)}) collective-permute-start(bf16[2,160,256]{2,1,0:T(8,128)(2,1)S(1)} %pad_maximum_fusion.2.keep), channel_id=1, source_target_pairs={{0,2},{2,0},{1,3},{3,1},{4,6},{6,4},{5,7},{7,5},{8,10},{10,8},{9,1... | collective-permute-start | bytes 491528 | tf_op jit(solution)/shard_map/ppermute | solution.py:19
  32.0 7.8 %collective-permute-done.8.refs_1_ = bf16[2,160,256]{2,1,0:T(8,128)(2,1)S(1)} collective-permute-done((bf16[2,160,256]{2,1,0:T(8,128)(2,1)S(1)}, bf16[2,160,256]{2,1,0:T(8,128)(2,1)S(1)}, u32[]{:S(2)}, u32[]{:S(2)}) %collective-permute-start.8) | collective-permute-done | bytes 163872 | tf_op jit(solution)/shard_map/ppermute | solution.py:54
  46.3 7.1 %solve.1 = (bf16[640,256]{1,0:T(8,128)(2,1)S(1)}, bf16[640,256]{1,0:T(8,128)(2,1)S(1)}, bf16[2,2,160,128]{3,2,1,0:T(8,128)(2,1)S(1)}, bf16[2,2,160,128]{3,2,1,0:...) custom-call(s32[11]{0:T(128)S(1)} %concatenate.30.meta, ...), custom_call_target="tpu_custom_call" | custom-call | tf_op jit(solution)/shard_map/solve/pallas_call | solution.py:275
  54.0 1.5 %collective-permute-start.17 = (bf16[2,2,160,128]{3,2,1,0:T(8,128)(2,1)S(1)}, bf16[2,2,160,128]{3,2,1,0:T(8,128)(2,1)S(1)}, u32[]{:S(2)}, u32[]{:S(2)}) collective-permute-start(bf16[2,2,160,128]{3,2,1,0:T(8,128)(2,1)S(1)} %get-tuple-element.14), channel_id=1, source_target_pairs={{0,2},{2,0},{1,3},{3,1},{4,6},{6,4},{5,7},{7,5},{8,10},{10,8},{9,1... | collective-permute-start | bytes 491528 | tf_op jit(solution)/shard_map/ppermute | solution.py:19
  55.6 1.7 %collective-permute-start.13 = (bf16[2,2,160,128]{3,2,1,0:T(8,128)(2,1)S(1)}, bf16[2,2,160,128]{3,2,1,0:T(8,128)(2,1)S(1)}, u32[]{:S(2)}, u32[]{:S(2)}) collective-permute-start(bf16[2,2,160,128]{3,2,1,0:T(8,128)(2,1)S(1)} %get-tuple-element.23), channel_id=1, source_target_pairs={{0,4},{1,25},{2,6},{3,27},{4,0},{5,29},{6,2},{7,31},{8,12},{9,17},... | collective-permute-start | bytes 491528 | tf_op jit(solution)/shard_map/ppermute | solution.py:54
  58.9 1.4 %collective-permute-done.17 = bf16[2,2,160,128]{3,2,1,0:T(8,128)(2,1)S(1)} collective-permute-done((bf16[2,2,160,128]{3,2,1,0:T(8,128)(2,1)S(1)}, bf16[2,2,160,128]{3,2,1,0:T(8,128)(2,1)S(1)}, u32[]{:S(2)}, u32[]{:S(2)}) %collective-permute-start.17) | collective-permute-done | bytes 163872 | tf_op jit(solution)/shard_map/ppermute | solution.py:19
  60.3 3.9 %collective-permute-done.19 = bf16[2,2,160,128]{3,2,1,0:T(8,128)(2,1)S(1)} collective-permute-done((bf16[2,2,160,128]{3,2,1,0:T(8,128)(2,1)S(1)}, bf16[2,2,160,128]{3,2,1,0:T(8,128)(2,1)S(1)}, u32[]{:S(2)}, u32[]{:S(2)}) %collective-permute-start.19) | collective-permute-done | bytes 163872 | tf_op jit(solution)/shard_map/ppermute | solution.py:19
  64.3 3.2 %collective-permute-start.20 = (bf16[2,2,160,128]{3,2,1,0:T(8,128)(2,1)S(1)}, bf16[2,2,160,128]{3,2,1,0:T(8,128)(2,1)S(1)}, u32[]{:S(2)}, u32[]{:S(2)}) collective-permute-start(bf16[2,2,160,128]{3,2,1,0:T(8,128)(2,1)S(1)} %get-tuple-element.21), channel_id=1, source_target_pairs={{0,16},{1,13},{2,18},{3,15},{4,20},{5,9},{6,22},{7,11},{8,24},{9,5... | collective-permute-start | bytes 491528 | tf_op jit(solution)/shard_map/ppermute | solution.py:54
  67.7 2.0 %collective-permute-start.14 = (bf16[2,2,160,128]{3,2,1,0:T(8,128)(2,1)S(1)}, bf16[2,2,160,128]{3,2,1,0:T(8,128)(2,1)S(1)}, u32[]{:S(2)}, u32[]{:S(2)}) collective-permute-start(bf16[2,2,160,128]{3,2,1,0:T(8,128)(2,1)S(1)} %pad_maximum_fusion.5.keep), channel_id=1, source_target_pairs={{0,2},{2,0},{1,3},{3,1},{4,6},{6,4},{5,7},{7,5},{8,10},{10,8},{9,1... | collective-permute-start | bytes 491528 | tf_op jit(solution)/shard_map/ppermute | solution.py:19
  69.7 6.2 %collective-permute-done.21.refs_1_ = bf16[2,2,160,128]{3,2,1,0:T(8,128)(2,1)S(1)} collective-permute-done((bf16[2,2,160,128]{3,2,1,0:T(8,128)(2,1)S(1)}, bf16[2,2,160,128]{3,2,1,0:T(8,128)(2,1)S(1)}, u32[]{:S(2)}, u32[]{:S(2)}) %collective-permute-start.21) | collective-permute-done | bytes 163872 | tf_op jit(solution)/shard_map/ppermute | solution.py:54
  77.0 1.6 %collective-permute-start.16 = (bf16[2,2,160,128]{3,2,1,0:T(8,128)(2,1)S(1)}, bf16[2,2,160,128]{3,2,1,0:T(8,128)(2,1)S(1)}, u32[]{:S(2)}, u32[]{:S(2)}) collective-permute-start(bf16[2,2,160,128]{3,2,1,0:T(8,128)(2,1)S(1)} %collective-permute-done.15.got), channel_id=1, source_target_pairs={{0,2},{2,0},{1,3},{3,1},{4,6},{6,4},{5,7},{7,5},{8,10},{10,8},{9,1... | collective-permute-start | bytes 491528 | tf_op jit(solution)/shard_map/ppermute | solution.py:19
  79.6 2.8 %collective-permute-done.16.got_peer = bf16[2,2,160,128]{3,2,1,0:T(8,128)(2,1)S(1)} collective-permute-done((bf16[2,2,160,128]{3,2,1,0:T(8,128)(2,1)S(1)}, bf16[2,2,160,128]{3,2,1,0:T(8,128)(2,1)S(1)}, u32[]{:S(2)}, u32[]{:S(2)}) %collective-permute-start.16) | collective-permute-done | bytes 163872 | tf_op jit(solution)/shard_map/ppermute | solution.py:19
  82.4 2.2 %place.1 = bf16[160,16,128]{2,1,0:T(8,128)(2,1)} custom-call(s32[11]{0:T(128)S(1)} %concatenate.30.meta, s32[16]{0:T(128)S(1)} %copy-done.11, bf16[2,2,160,128]{3,2,1,0:T(8,128)(2,1)S(1)} %pad_maximum_fusion.5.keep, bf16[2,2,160,128]{3,2,1,0:T(8,128)(2,1)S(1)} %collective-permute-done.14.keep_peer, bf16[2,2,160,128]{3,2,1,0:T(8,128)(2,1)S(1)} %collective-permute-done.15.got, ...), custom_call_target="tpu_custom_call" | custom-call | tf_op jit(solution)/shard_map/place/pallas_call | solution.py:314
  (83 shorter events, 17.6 us)
Async XLA Ops:
  0.6 2.5 %collective-permute-start = (bf16[160,16,128]{2,1,0:T(8,128)(2,1)}, bf16[160,16,128]{2,1,0:T(8,128)(2,1)S(1)}, u32[]{:S(2)}, u32[]{:S(2)}) collective-permute-start(bf16[160,16,128]{2,1,0:T(8,128)(2,1)} %bitcast.38), channel_id=1, source_target_pairs={{0,1},{1,0},{2,3},{3,2},{4,5},{5,4},{6,7},{7,6},{8,9},{9,8},{10,11... | collective-permute-start | bytes 1966088 | tf_op jit(solution)/shard_map/ppermute | solution.py:19
  7.1 11.1 %collective-permute-start.1 = (bf16[2,160,256]{2,1,0:T(8,128)(2,1)S(1)}, bf16[2,160,256]{2,1,0:T(8,128)(2,1)}, u32[]{:S(2)}, u32[]{:S(2)}) collective-permute-start(bf16[2,160,256]{2,1,0:T(8,128)(2,1)S(1)} %get-tuple-element.26), channel_id=1, source_target_pairs={{1,9},{3,11},{5,13},{7,15},{9,1},{11,3},{13,5},{15,7},{17,25},{19,... | collective-permute-start | bytes 491528 | tf_op jit(solution)/shard_map/ppermute | solution.py:54
  11.8 31.9 %collective-permute-start.10 = (bf16[640,1280]{1,0:T(8,128)(2,1)}, bf16[640,1280]{1,0:T(8,128)(2,1)S(1)}, u32[]{:S(2)}, u32[]{:S(2)}) collective-permute-start(bf16[640,1280]{1,0:T(8,128)(2,1)} %get-tuple-element.18), channel_id=1, source_target_pairs={{0,1},{1,0},{2,3},{3,2},{4,5},{5,4},{6,7},{7,6},{8,9},{9,8},{10,11... | collective-permute-start | bytes 4915208 | tf_op jit(solution)/shard_map/ppermute | solution.py:19
  15.2 5.5 %collective-permute-start.2 = (bf16[2,160,256]{2,1,0:T(8,128)(2,1)}, bf16[2,160,256]{2,1,0:T(8,128)(2,1)S(1)}, u32[]{:S(2)}, u32[]{:S(2)}) collective-permute-start(bf16[2,160,256]{2,1,0:T(8,128)(2,1)} %get-tuple-element.27), channel_id=1, source_target_pairs={{0,4},{1,25},{2,6},{3,27},{4,0},{5,29},{6,2},{7,31},{8,12},{9,17},... | collective-permute-start | bytes 491528 | tf_op jit(solution)/shard_map/ppermute | solution.py:54
  16.6 10.5 %collective-permute-start.6 = (bf16[2,2,160,256]{3,2,1,0:T(8,128)(2,1)}, bf16[2,2,160,256]{3,2,1,0:T(8,128)(2,1)S(1)}, u32[]{:S(2)}, u32[]{:S(2)}) collective-permute-start(bf16[2,2,160,256]{3,2,1,0:T(8,128)(2,1)} %copy-done.6), channel_id=1, source_target_pairs={{0,2},{2,0},{1,3},{3,1},{4,6},{6,4},{5,7},{7,5},{8,10},{10,8},{9,1... | collective-permute-start | bytes 983048 | tf_op jit(solution)/shard_map/ppermute | solution.py:19
  20.7 10.8 %collective-permute-start.4 = (bf16[2,160,256]{2,1,0:T(8,128)(2,1)S(1)}, bf16[2,160,256]{2,1,0:T(8,128)(2,1)}, u32[]{:S(2)}, u32[]{:S(2)}) collective-permute-start(bf16[2,160,256]{2,1,0:T(8,128)(2,1)S(1)} %pad_maximum_fusion.3), channel_id=1, source_target_pairs={{0,1},{1,0},{2,3},{3,2},{4,5},{5,4},{6,7},{7,6},{8,9},{9,8},{10,11... | collective-permute-start | bytes 491528 | tf_op jit(solution)/shard_map/ppermute | solution.py:19
  27.3 12.5 %collective-permute-start.8 = (bf16[2,160,256]{2,1,0:T(8,128)(2,1)S(1)}, bf16[2,160,256]{2,1,0:T(8,128)(2,1)S(1)}, u32[]{:S(2)}, u32[]{:S(2)}) collective-permute-start(bf16[2,160,256]{2,1,0:T(8,128)(2,1)S(1)} %get-tuple-element.24), channel_id=1, source_target_pairs={{0,20},{1,29},{2,22},{3,31},{4,16},{5,25},{6,18},{7,27},{8,28},{9,... | collective-permute-start | bytes 491528 | tf_op jit(solution)/shard_map/ppermute | solution.py:54
  28.8 11.7 %collective-permute-start.7 = (bf16[2,160,256]{2,1,0:T(8,128)(2,1)S(1)}, bf16[2,160,256]{2,1,0:T(8,128)(2,1)S(1)}, u32[]{:S(2)}, u32[]{:S(2)}) collective-permute-start(bf16[2,160,256]{2,1,0:T(8,128)(2,1)S(1)} %get-tuple-element.25), channel_id=1, source_target_pairs={{0,16},{1,13},{2,18},{3,15},{4,20},{5,9},{6,22},{7,11},{8,24},{9,5... | collective-permute-start | bytes 491528 | tf_op jit(solution)/shard_map/ppermute | solution.py:54
  29.9 13.3 %collective-permute-start.3 = (bf16[2,160,256]{2,1,0:T(8,128)(2,1)S(1)}, bf16[2,160,256]{2,1,0:T(8,128)(2,1)}, u32[]{:S(2)}, u32[]{:S(2)}) collective-permute-start(bf16[2,160,256]{2,1,0:T(8,128)(2,1)S(1)} %pad_maximum_fusion.2.keep), channel_id=1, source_target_pairs={{0,2},{2,0},{1,3},{3,1},{4,6},{6,4},{5,7},{7,5},{8,10},{10,8},{9,1... | collective-permute-start | bytes 491528 | tf_op jit(solution)/shard_map/ppermute | solution.py:19
  31.5 11.7 %collective-permute-start.5 = (bf16[2,160,256]{2,1,0:T(8,128)(2,1)}, bf16[2,160,256]{2,1,0:T(8,128)(2,1)}, u32[]{:S(2)}, u32[]{:S(2)}) collective-permute-start(bf16[2,160,256]{2,1,0:T(8,128)(2,1)} %collective-permute-done.4.got), channel_id=1, source_target_pairs={{0,2},{2,0},{1,3},{3,1},{4,6},{6,4},{5,7},{7,5},{8,10},{10,8},{9,1... | collective-permute-start | bytes 491528 | tf_op jit(solution)/shard_map/ppermute | solution.py:19
  41.9 1.7 %collective-permute-start.9 = (bf16[2,160,256]{2,1,0:T(8,128)(2,1)}, bf16[2,160,256]{2,1,0:T(8,128)(2,1)}, u32[]{:S(2)}, u32[]{:S(2)}) collective-permute-start(bf16[2,160,256]{2,1,0:T(8,128)(2,1)} %pad_maximum_fusion.4), channel_id=1, source_target_pairs={{0,1},{1,0},{2,3},{3,2},{4,5},{5,4},{6,7},{7,6},{8,9},{9,8},{10,11... | collective-permute-start | bytes 491528 | tf_op jit(solution)/shard_map/ppermute | solution.py:19
  53.4 2.1 %collective-permute-start.11 = (bf16[2,2,160,128]{3,2,1,0:T(8,128)(2,1)S(1)}, bf16[2,2,160,128]{3,2,1,0:T(8,128)(2,1)S(1)}, u32[]{:S(2)}, u32[]{:S(2)}) collective-permute-start(bf16[2,2,160,128]{3,2,1,0:T(8,128)(2,1)S(1)} %get-tuple-element.13), channel_id=1, source_target_pairs={{0,1},{1,0},{2,3},{3,2},{4,5},{5,4},{6,7},{7,6},{8,9},{9,8},{10,11... | collective-permute-start | bytes 491528 | tf_op jit(solution)/shard_map/ppermute | solution.py:19
  53.6 4.3 %collective-permute-start.18 = (bf16[2,2,160,128]{3,2,1,0:T(8,128)(2,1)S(1)}, bf16[2,2,160,128]{3,2,1,0:T(8,128)(2,1)S(1)}, u32[]{:S(2)}, u32[]{:S(2)}) collective-permute-start(bf16[2,2,160,128]{3,2,1,0:T(8,128)(2,1)S(1)} %get-tuple-element.15), channel_id=1, source_target_pairs={{0,1},{1,0},{2,3},{3,2},{4,5},{5,4},{6,7},{7,6},{8,9},{9,8},{10,11... | collective-permute-start | bytes 491528 | tf_op jit(solution)/shard_map/ppermute | solution.py:19
  54.0 6.2 %collective-permute-start.17 = (bf16[2,2,160,128]{3,2,1,0:T(8,128)(2,1)S(1)}, bf16[2,2,160,128]{3,2,1,0:T(8,128)(2,1)S(1)}, u32[]{:S(2)}, u32[]{:S(2)}) collective-permute-start(bf16[2,2,160,128]{3,2,1,0:T(8,128)(2,1)S(1)} %get-tuple-element.14), channel_id=1, source_target_pairs={{0,2},{2,0},{1,3},{3,1},{4,6},{6,4},{5,7},{7,5},{8,10},{10,8},{9,1... | collective-permute-start | bytes 491528 | tf_op jit(solution)/shard_map/ppermute | solution.py:19
  55.5 23.1 %collective-permute-start.23 = (bf16[640,256]{1,0:T(8,128)(2,1)S(1)}, bf16[640,256]{1,0:T(8,128)(2,1)S(1)}, u32[]{:S(2)}, u32[]{:S(2)}) collective-permute-start(bf16[640,256]{1,0:T(8,128)(2,1)S(1)} %get-tuple-element.17), channel_id=1, source_target_pairs={{0,1},{1,0},{2,3},{3,2},{4,5},{5,4},{6,7},{7,6},{8,9},{9,8},{10,11... | collective-permute-start | bytes 983048 | tf_op jit(solution)/shard_map/ppermute | solution.py:19
  55.6 12.0 %collective-permute-start.13 = (bf16[2,2,160,128]{3,2,1,0:T(8,128)(2,1)S(1)}, bf16[2,2,160,128]{3,2,1,0:T(8,128)(2,1)S(1)}, u32[]{:S(2)}, u32[]{:S(2)}) collective-permute-start(bf16[2,2,160,128]{3,2,1,0:T(8,128)(2,1)S(1)} %get-tuple-element.23), channel_id=1, source_target_pairs={{0,4},{1,25},{2,6},{3,27},{4,0},{5,29},{6,2},{7,31},{8,12},{9,17},... | collective-permute-start | bytes 491528 | tf_op jit(solution)/shard_map/ppermute | solution.py:54
  57.3 10.2 %collective-permute-start.12 = (bf16[2,2,160,128]{3,2,1,0:T(8,128)(2,1)S(1)}, bf16[2,2,160,128]{3,2,1,0:T(8,128)(2,1)S(1)}, u32[]{:S(2)}, u32[]{:S(2)}) collective-permute-start(bf16[2,2,160,128]{3,2,1,0:T(8,128)(2,1)S(1)} %get-tuple-element.22), channel_id=1, source_target_pairs={{1,9},{3,11},{5,13},{7,15},{9,1},{11,3},{13,5},{15,7},{17,25},{19,... | collective-permute-start | bytes 491528 | tf_op jit(solution)/shard_map/ppermute | solution.py:54
  57.9 6.2 %collective-permute-start.19 = (bf16[2,2,160,128]{3,2,1,0:T(8,128)(2,1)S(1)}, bf16[2,2,160,128]{3,2,1,0:T(8,128)(2,1)S(1)}, u32[]{:S(2)}, u32[]{:S(2)}) collective-permute-start(bf16[2,2,160,128]{3,2,1,0:T(8,128)(2,1)S(1)} %collective-permute-done.18), channel_id=1, source_target_pairs={{0,2},{2,0},{1,3},{3,1},{4,6},{6,4},{5,7},{7,5},{8,10},{10,8},{9,1... | collective-permute-start | bytes 491528 | tf_op jit(solution)/shard_map/ppermute | solution.py:19
  64.3 11.7 %collective-permute-start.21 = (bf16[2,2,160,128]{3,2,1,0:T(8,128)(2,1)S(1)}, bf16[2,2,160,128]{3,2,1,0:T(8,128)(2,1)S(1)}, u32[]{:S(2)}, u32[]{:S(2)}) collective-permute-start(bf16[2,2,160,128]{3,2,1,0:T(8,128)(2,1)S(1)} %get-tuple-element.20), channel_id=1, source_target_pairs={{0,20},{1,29},{2,22},{3,31},{4,16},{5,25},{6,18},{7,27},{8,28},{9,... | collective-permute-start | bytes 491528 | tf_op jit(solution)/shard_map/ppermute | solution.py:54
  64.3 12.7 %collective-permute-start.20 = (bf16[2,2,160,128]{3,2,1,0:T(8,128)(2,1)S(1)}, bf16[2,2,160,128]{3,2,1,0:T(8,128)(2,1)S(1)}, u32[]{:S(2)}, u32[]{:S(2)}) collective-permute-start(bf16[2,2,160,128]{3,2,1,0:T(8,128)(2,1)S(1)} %get-tuple-element.21), channel_id=1, source_target_pairs={{0,16},{1,13},{2,18},{3,15},{4,20},{5,9},{6,22},{7,11},{8,24},{9,5... | collective-permute-start | bytes 491528 | tf_op jit(solution)/shard_map/ppermute | solution.py:54
  67.6 9.4 %collective-permute-start.15 = (bf16[2,2,160,128]{3,2,1,0:T(8,128)(2,1)S(1)}, bf16[2,2,160,128]{3,2,1,0:T(8,128)(2,1)S(1)}, u32[]{:S(2)}, u32[]{:S(2)}) collective-permute-start(bf16[2,2,160,128]{3,2,1,0:T(8,128)(2,1)S(1)} %pad_maximum_fusion.6), channel_id=1, source_target_pairs={{0,1},{1,0},{2,3},{3,2},{4,5},{5,4},{6,7},{7,6},{8,9},{9,8},{10,11... | collective-permute-start | bytes 491528 | tf_op jit(solution)/shard_map/ppermute | solution.py:19
  67.7 11.9 %collective-permute-start.14 = (bf16[2,2,160,128]{3,2,1,0:T(8,128)(2,1)S(1)}, bf16[2,2,160,128]{3,2,1,0:T(8,128)(2,1)S(1)}, u32[]{:S(2)}, u32[]{:S(2)}) collective-permute-start(bf16[2,2,160,128]{3,2,1,0:T(8,128)(2,1)S(1)} %pad_maximum_fusion.5.keep), channel_id=1, source_target_pairs={{0,2},{2,0},{1,3},{3,1},{4,6},{6,4},{5,7},{7,5},{8,10},{10,8},{9,1... | collective-permute-start | bytes 491528 | tf_op jit(solution)/shard_map/ppermute | solution.py:19
  77.0 5.4 %collective-permute-start.16 = (bf16[2,2,160,128]{3,2,1,0:T(8,128)(2,1)S(1)}, bf16[2,2,160,128]{3,2,1,0:T(8,128)(2,1)S(1)}, u32[]{:S(2)}, u32[]{:S(2)}) collective-permute-start(bf16[2,2,160,128]{3,2,1,0:T(8,128)(2,1)S(1)} %collective-permute-done.15.got), channel_id=1, source_target_pairs={{0,2},{2,0},{1,3},{3,1},{4,6},{6,4},{5,7},{7,5},{8,10},{10,8},{9,1... | collective-permute-start | bytes 491528 | tf_op jit(solution)/shard_map/ppermute | solution.py:19
  78.6 3.8 %collective-permute-start.22 = (bf16[2,2,160,128]{3,2,1,0:T(8,128)(2,1)S(1)}, bf16[2,2,160,128]{3,2,1,0:T(8,128)(2,1)S(1)}, u32[]{:S(2)}, u32[]{:S(2)}) collective-permute-start(bf16[2,2,160,128]{3,2,1,0:T(8,128)(2,1)S(1)} %pad_maximum_fusion.7), channel_id=1, source_target_pairs={{0,1},{1,0},{2,3},{3,2},{4,5},{5,4},{6,7},{7,6},{8,9},{9,8},{10,11... | collective-permute-start | bytes 491528 | tf_op jit(solution)/shard_map/ppermute | solution.py:19
  (13 other events, 91.2 us)

commit v2 on v0

--- a/solution.py
+++ b/solution.py
@@ -1,7 +1,17 @@
+import functools
+
 import jax
 import jax.numpy as jnp
 from jax import lax
+from jax.experimental import pallas as pl
+from jax.experimental.pallas import tpu as pltpu
 from jax.sharding import PartitionSpec as P
+
+AXES = ("wave", "parity", "lev")
+VMEM = pl.BlockSpec(memory_space=pltpu.VMEM)
+SMEM = pl.BlockSpec(memory_space=pltpu.SMEM)
+HBM = pl.BlockSpec(memory_space=pltpu.HBM)
+MIB = 1024 * 1024
 
 
 def partner_2(value, axis, distance):
@@ -16,13 +26,396 @@
     )
 
 
+RAW_STEPS = 1
+
+
+def mask_plan(owners):
+    even = range(owners - 2, -1, -2)
+    cores = [
+        [mask + (1 - core if step < RAW_STEPS else core) for step, mask in enumerate(even)]
+        for core in range(2)
+    ]
+    return [masks[RAW_STEPS:] for masks in cores], [masks[:RAW_STEPS] for masks in cores]
+
+
+def swap(value, axis):
+    return lax.ppermute(value, axis, [(0, 1), (1, 0)])
+
+
+def meet(value, masks):
+    owners, hemis = lax.axis_size("wave"), lax.axis_size("parity")
+    pairs = []
+    for wave in range(owners):
+        for hemi in range(hemis):
+            for core, mask in enumerate(masks):
+                if mask:
+                    source = (wave * hemis + hemi) * 2 + core
+                    target = ((wave ^ mask) * hemis + hemi) * 2 + core
+                    pairs.append((source, target))
+    return lax.ppermute(value, AXES, pairs)
+
+
+def here():
+    return tuple(lax.axis_index(axis).astype(jnp.int32) for axis in AXES)
+
+
+def owner_met(masks, index, wave, core):
+    return wave ^ jnp.where(core == 0, masks[0][index], masks[1][index])
+
+
+def fold_with(sign):
+    def fold(own, peer):
+        return (peer.astype(jnp.float32) + sign * own.astype(jnp.float32)).astype(jnp.bfloat16)
+
+    return fold
+
+
+def parity_sign(parity):
+    return (1 - 2 * parity).astype(jnp.float32)
+
+
+def join_kernel(mine, got, *outs):
+    for i, out in enumerate(outs):
+        out[:, 0] = mine[i]
+        out[:, 1] = got[i]
+
+
+def fold_kernel(own, peer, out):
+    out[...] = fold_with(parity_sign(here()[1]))(own[...], peer[...])
+
+
+def gather_kernel(*refs, folds, raws):
+    raw, folded, (sent, keep, give) = refs[:raws], refs[raws:-3], refs[-3:]
+    lev = here()[2]
+    for part, out in enumerate((keep, give)):
+        for i in range(folds):
+            value = folded[i][part]
+            if i == folds - 1:
+                value = jnp.where(lev == 0, sent[part], value)
+            out[i] = value
+        for i in range(raws):
+            out[folds + i] = raw[i][part]
+
+
+def exchange(fold_mine, fold_other, raw_mine, raw_other, aside, plan):
+    folds, _, rows, side = fold_mine.shape
+    raws = raw_mine.shape[0]
+    fold_masks, raw_masks = plan
+    block = jax.ShapeDtypeStruct((2, 2, rows, side), jnp.bfloat16)
+    fold = call(fold_kernel, block, "fold", 8)
+    raw_got = swap(raw_other, "lev")
+    fold_got = swap(fold_other, "lev")
+    raw_sent = call(join_kernel, (block,) * raws, "join", 8)(raw_mine, raw_got)
+    raw = [meet(b, (raw_masks[0][i], raw_masks[1][i])) for i, b in enumerate(raw_sent)]
+    raw_folded = [fold(b, swap(b, "parity")) for b in raw]
+    aside = aside((fold_got, raw_got))
+    plain = call(join_kernel, (block,) * folds, "join", 8)(fold_mine, fold_got)
+    sent = [fold(b, swap(b, "parity")) for b in plain]
+    folded = [meet(b, (fold_masks[0][i], fold_masks[1][i])) for i, b in enumerate(sent)]
+    last, aside = lax.optimization_barrier((sent[-1], aside))
+    whole = jax.ShapeDtypeStruct((folds + raws, 2, rows, side), jnp.bfloat16)
+    keep, give = call(
+        functools.partial(gather_kernel, folds=folds, raws=raws), (whole, whole), "gather", 8
+    )(*raw_folded, *folded, last)
+    return keep, swap(give, "lev"), aside
+
+
+def call(kernel, shapes, name, mebibytes, scratch=(), in_specs=None, out_spec=VMEM):
+    def run(*args):
+        moved = sum(a.size * a.dtype.itemsize for a in (*args, *jax.tree.leaves(shapes)))
+        return pl.pallas_call(
+            kernel,
+            out_shape=shapes,
+            in_specs=in_specs or [VMEM] * len(args),
+            out_specs=jax.tree.map(lambda _: out_spec, shapes),
+            scratch_shapes=scratch,
+            cost_estimate=pl.CostEstimate(flops=0, bytes_accessed=moved, transcendentals=0),
+            compiler_params=pltpu.CompilerParams(vmem_limit_bytes=mebibytes * MIB),
+            name=name,
+        )(*args)
+
+    return run
+
+
+def send_order(plan, wave, lev):
+    order = []
+    for group, masks in enumerate(plan):
+        for i in range(len(masks[0])):
+            for other in range(2):
+                core = 1 - lev if other else lev
+                order.append((2 * group + other, i, owner_met(masks, i, wave, core), core))
+    return order
+
+
+def arrival_order(plan, wave, lev):
+    order = []
+    for other in range(2):
+        core = 1 - lev if other else lev
+        at = 0
+        for masks in plan:
+            for i in range(len(masks[0])):
+                order.append((other, at, owner_met(masks, i, wave, core), core))
+                at += 1
+    return order
+
+
+def wave_order(slots, waves, group):
+    size = waves * group
+    row = lax.broadcasted_iota(jnp.int32, (group, size), 0)
+    column = lax.broadcasted_iota(jnp.int32, (group, size), 1)
+    return jnp.concatenate(
+        [(column == row * waves + slots[slot]).astype(jnp.bfloat16) for slot in range(waves)]
+    )
+
+
+def scale_kernel(slots_hbm, grid_hbm, weights_hbm, *refs, plan):
+    outs, (slots, grid, weights, wide, held, done) = refs[:4], refs[4:]
+    rows, waves, side = grid.shape
+    group = wide.shape[0] // waves
+    groups = rows // group
+    wave, _, lev = here()
+    cuts = 2
+    step = groups // cuts
+    copies = [
+        pltpu.make_async_copy(slots_hbm, slots, done.at[0]),
+        pltpu.make_async_copy(weights_hbm, weights, done.at[1]),
+    ]
+    for i in range(cuts):
+        at = pl.ds(i * step * group, step * group)
+        copies.append(pltpu.make_async_copy(grid_hbm.at[at], grid.at[at], done.at[2 + i]))
+    for copy in copies:
+        copy.start()
+    copies[0].wait()
+    order = wave_order(slots, waves, group)
+    copies[1].wait()
+    scale = jnp.transpose(jnp.broadcast_to(weights[...], (side, rows)))
+    for cut in range(cuts):
+        copies[2 + cut].wait()
+        for i in range(cut * step, (cut + 1) * step):
+            wide[:, i * side : (i + 1) * side] = grid[i * group : (i + 1) * group].reshape(
+                group * waves, side
+            )
+        span = slice(cut * step * side, (cut + 1) * step * side)
+        picked = jnp.dot(order, wide[:, span], preferred_element_type=jnp.float32)
+        for i in range(step):
+            at = slice((cut * step + i) * group, (cut * step + i + 1) * group)
+            for slot in range(waves):
+                held[slot, at] = (
+                    scale[at]
+                    * picked[slot * group : (slot + 1) * group, i * side : (i + 1) * side]
+                ).astype(jnp.bfloat16)
+    for out, i, owner, core in send_order(plan, wave, lev):
+        outs[out][i, 0] = held[2 * owner + core]
+        outs[out][i, 1] = held[2 * owner + 1 - core]
+
+
+def lanes(index, side):
+    return pl.ds(pl.multiple_of(index * side, side), side)
+
+
+def widen_kernel(to_modes, from_modes, rates, to_wide, from_wide, rate):
+    levels = to_modes.shape[0]
+    width = 2 * levels
+    bf16, f32 = jnp.bfloat16, jnp.float32
+    spread = (
+        (lax.broadcasted_iota(jnp.int32, (width, levels), 0) >> 1)
+        == lax.broadcasted_iota(jnp.int32, (width, levels), 1)
+    ).astype(f32)
+    spread_16 = spread.astype(bf16)
+    row = lax.broadcasted_iota(jnp.int32, (width, width), 0)
+    column = lax.broadcasted_iota(jnp.int32, (width, width), 1)
+    same = ((row + column) & 1) == 0
+
+    def widen(square):
+        tall = jnp.dot(spread_16, square, preferred_element_type=f32).astype(bf16)
+        wide = lax.dot_general(
+            tall, spread_16, (((1,), (1,)), ((), ())), preferred_element_type=f32
+        )
+        return jnp.where(same, wide, 0.0).astype(bf16)
+
+    for square, out in ((to_modes, to_wide), (from_modes, from_wide)):
+        high = square[...].astype(bf16)
+        low = (square[...] - high.astype(f32)).astype(bf16)
+        wide = widen(high)
+        out[:, 0:width] = wide
+        out[:, width : 2 * width] = wide
+        out[:, 2 * width :] = widen(low)
+    rate[...] = jnp.sum(spread * rates[...], axis=1, keepdims=True)
+
+
+def product_3(wide, value):
+    high = value.astype(jnp.bfloat16)
+    low = (value - high.astype(jnp.float32)).astype(jnp.bfloat16)
+    return jnp.dot(
+        wide[...], jnp.concatenate([high, low, high], axis=0), preferred_element_type=jnp.float32
+    )
+
+
+def solve_kernel(
+    slots, keep, got, tables_mine, tables_other, to_wide, from_wide, rate, *refs, plan
+):
+    (spec_mine, spec_other), outs, (data, spec, parts) = refs[:2], refs[2:6], refs[6:]
+    wave, parity, lev = here()
+    rows, side = keep.shape[2:]
+    half, degrees = tables_mine.shape[2:]
+    table_mine, table_other = tables_mine.at[lev, 0], tables_other.at[lev, 0]
+
+    def place(owner):
+        return pl.ds(pl.multiple_of(owner * rows, 16), rows)
+
+    for other, index, owner, core in arrival_order(plan, wave, lev):
+        block = got if other else keep
+        data[place(owner), lanes(core, side)] = block[index, 0]
+        data[place(owner), lanes(1 - core, side)] = block[index, 1]
+    at_mine = pl.ds(pl.multiple_of(lev * half, 16), half)
+    at_other = pl.ds(pl.multiple_of((1 - lev) * half, 16), half)
+    rows_first = (((0,), (0,)), ((), ()))
+    raw = lax.dot_general(
+        data[at_mine, :], table_mine[...], rows_first, preferred_element_type=jnp.float32
+    ) + lax.dot_general(
+        data[at_other, :], table_other[...], rows_first, preferred_element_type=jnp.float32
+    )
+    top_degree = 2 * degrees - 1
+    degree = (
+        slots[2 * wave + lev] + parity + 2 * lax.broadcasted_iota(jnp.int32, (1, degrees), 1)
+    )
+    kept = jnp.where(degree <= top_degree, raw, 0.0)
+    degree_f = degree.astype(jnp.float32)
+    stiffness = degree_f * (degree_f + 1.0) / (top_degree * (top_degree + 1.0))
+    damped = product_3(to_wide, kept) / (1.0 + stiffness * rate[...])
+    updated = product_3(from_wide, damped)
+    spec[...] = jnp.transpose(updated.astype(jnp.bfloat16))
+    for at, table in ((at_mine, table_mine), (at_other, table_other)):
+        parts[at, :] = jnp.dot(
+            table[...], spec[...], preferred_element_type=jnp.float32
+        ).astype(jnp.bfloat16)
+    spec_mine[...] = spec[at_mine, :]
+    spec_other[...] = spec[at_other, :]
+    for out, i, owner, core in send_order(plan, wave, lev):
+        outs[out][i, 0] = parts[place(owner), lanes(core, side)]
+        outs[out][i, 1] = parts[place(owner), lanes(1 - core, side)]
+
+
+def place_kernel(slots, keep, got, spec_mine, spec_got, columns, spectral, *refs, plan):
+    held, wide, ready, done = refs
+    rows, waves, side = ready.shape
+    group = wide.shape[0] // waves
+    groups = rows // group
+    wave, _, lev = here()
+    width = spec_mine.shape[1]
+    copies = [
+        pltpu.make_async_copy(half, spectral.at[:, lanes(core, width)], done.at[i])
+        for i, (half, core) in enumerate(((spec_mine, lev), (spec_got, 1 - lev)))
+    ]
+    for copy in copies:
+        copy.start()
+    for other, index, owner, core in arrival_order(plan, wave, lev):
+        block = got if other else keep
+        held[2 * owner + core] = block[index, 0]
+        held[2 * owner + 1 - core] = block[index, 1]
+    order = wave_order(slots, waves, group)
+    cuts = done.shape[0] - 2
+    step = groups // cuts
+    for cut in range(cuts):
+        for i in range(cut * step, (cut + 1) * step):
+            for slot in range(waves):
+                wide[slot * group : (slot + 1) * group, i * side : (i + 1) * side] = held[
+                    slot, i * group : (i + 1) * group
+                ]
+        span = slice(cut * step * side, (cut + 1) * step * side)
+        placed = lax.dot_general(
+            order,
+            wide[:, span],
+            (((0,), (0,)), ((), ())),
+            preferred_element_type=jnp.float32,
+        ).astype(jnp.bfloat16)
+        for i in range(step):
+            ready[(cut * step + i) * group : (cut * step + i + 1) * group] = placed[
+                :, i * side : (i + 1) * side
+            ].reshape(group, waves, side)
+        at = pl.ds(cut * step * group, step * group)
+        copies.append(pltpu.make_async_copy(ready.at[at], columns.at[at], done.at[2 + cut]))
+        copies[-1].start()
+    for copy in copies:
+        copy.wait()
+
+
+def per_device(fourier, legendre, quad_weights, slot_wave, to_modes, from_modes, mode_rates):
+    plan = mask_plan(lax.axis_size("wave"))
+    rows, waves, side = fourier.shape[1:]
+    width = 2 * side
+    half, degrees = legendre.shape[2:]
+    bf16, f32 = jnp.bfloat16, jnp.float32
+    pieces = tuple(
+        jax.ShapeDtypeStruct((len(masks[0]), 2, rows, side), bf16) for masks in plan for _ in range(2)
+    )
+    group = 16
+    held = pltpu.VMEM((waves, rows, side), bf16)
+    wide_rows = pltpu.VMEM((group * waves, rows // group * side), bf16)
+
+    scaled = call(
+        functools.partial(scale_kernel, plan=plan),
+        pieces,
+        "scale",
+        48,
+        (
+            pltpu.SMEM(slot_wave.shape, jnp.int32),
+            pltpu.VMEM((rows, waves, side), bf16),
+            pltpu.VMEM((1, rows), f32),
+            wide_rows,
+            held,
+            pltpu.SemaphoreType.DMA((4,)),
+        ),
+        [HBM] * 3,
+    )(slot_wave, fourier[0], quad_weights[None, :])
+    keep, got, table_other = exchange(
+        *scaled, lambda tie: swap(lax.optimization_barrier((legendre, *tie))[0], "lev"), plan
+    )
+
+    wide = jax.ShapeDtypeStruct((width, 3 * width), bf16)
+    to_wide, from_wide, rate = call(
+        widen_kernel, (wide, wide, jax.ShapeDtypeStruct((width, 1), f32)), "widen", 8
+    )(to_modes, from_modes, mode_rates[None, :])
+    spec_shape = jax.ShapeDtypeStruct((half, width), bf16)
+    spec_mine, spec_other, *parts = call(
+        functools.partial(solve_kernel, plan=plan),
+        (spec_shape, spec_shape) + pieces,
+        "solve",
+        20,
+        (pltpu.VMEM((2 * half, width), bf16),) * 3,
+        [SMEM] + [VMEM] * 7,
+    )(slot_wave, keep, got, legendre, table_other, to_wide, from_wide, rate)
+    def swap_spectral(tie):
+        return swap(lax.optimization_barrier((spec_other, *tie))[0], "lev")
+
+    keep, got, spec_got = exchange(*parts, swap_spectral, plan)
+    columns, spectral = call(
+        functools.partial(place_kernel, plan=plan),
+        (
+            jax.ShapeDtypeStruct((rows, waves, side), bf16),
+            jax.ShapeDtypeStruct((half, 2 * width), bf16),
+        ),
+        "place",
+        16,
+        (
+            held,
+            wide_rows,
+            pltpu.VMEM((rows, waves, side), bf16),
+            pltpu.SemaphoreType.DMA((7,)),
+        ),
+        [SMEM] + [VMEM] * 4,
+        HBM,
+    )(slot_wave, keep, got, spec_mine, spec_got)
+    return (columns[None], spectral[None])
+
+
 def widen_matrix(square):
     levels = square.shape[0]
     pair_eye = jnp.eye(2, dtype=jnp.float32)
     return (square[:, None, :, None] * pair_eye[None, :, None, :]).reshape(2 * levels, 2 * levels)
 
 
-def per_device(fourier, legendre, quad_weights, slot_wave, to_modes, from_modes, mode_rates):
+def per_device_many(fourier, legendre, quad_weights, slot_wave, to_modes, from_modes, mode_rates):
     parity = lax.axis_index("parity")
     signed_one = (1 - 2 * parity).astype(jnp.float32)
     levels = to_modes.shape[0]
@@ -110,6 +503,11 @@
         P(),
     )
     out_specs = (P("parity", "wave", None, "lev"), P("parity", "lev", "wave"))
+    few = mesh.shape["wave"] in (8, 16) and mesh.shape["lev"] == mesh.shape["parity"] == 2
     return jax.shard_map(
-        per_device, mesh=mesh, in_specs=in_specs, out_specs=out_specs, check_vma=False
-    )
+        per_device if few else per_device_many,
+        mesh=mesh,
+        in_specs=in_specs,
+        out_specs=out_specs,
+        check_vma=False,
+    )

time: 184 us -> 61.8 us (0.34)
  local copies, waits for them, and re-layouts: 53.9 us -> 2.58 us
  waiting for transfers between devices: 59.9 us -> 23.8 us
  other arithmetic: 21.6 us -> 0 us
  between operations: 14.3 us -> 0.8 us
  starting transfers between devices: 14.1 us -> 25.9 us
  matrix products: 9.95 us -> 0 us
  blocking collectives: 8.78 us -> 0 us
  Pallas kernels: 0 us -> 8.47 us
    all_to_all x2 -> x0, waiting for transfers between devices: 33.3 us -> none  [the longest x1 17.1 us: per_device(): lax.all_to_all(lax.all_to_all(parts, 'lev', split_axis=2, concat_axis=1,...]
    mul x3 -> x0, local copies, waits for them, and re-layouts: 26 us -> none  [the longest x2 25.9 us: widen_matrix(): square[:, None, :, None] * pair_eye[None, :, None, :]]
    ppermute x2 -> x24, starting transfers between devices: 4.51 us -> 25.9 us  [the longest x8 14.5 us: meet(): return lax.ppermute(value, AXES, pairs)]
    mul x2 -> x0, other arithmetic: 12.3 us -> none  [the longest x1 12.3 us: widen_matrix(): square[:, None, :, None] * pair_eye[None, :, None, :]]
    all_to_all x8 -> x0, local copies, waits for them, and re-layouts: 12.3 us -> none  [the longest x3 6.55 us: per_device(): lax.all_to_all(parts, 'lev', split_axis=2, concat_axis=1, tiled=True)]
    dot_general x6 -> x0, matrix products: 9.95 us -> none  [the longest x2 3.03 us: per_device(): sums.append(jnp.dot(deg_block, coeffs, preferred_element_type=jnp.float32))]
    all_to_all x2 -> x0, starting transfers between devices: 9.58 us -> none  [the longest x1 6.03 us: per_device(): lax.all_to_all(by_slot, 'wave', split_axis=0, concat_axis=1, tiled=True)]
    all_to_all x2 -> x0, blocking collectives: 8.78 us -> none  [the longest x1 4.52 us: per_device(): lax.all_to_all(lax.all_to_all(by_slot, 'wave', split_axis=0, concat_axis=...]
  transfers between devices with their start and end apart: 5 -> 24, of which waited for: 4 -> 16; matrix products, arithmetic and copies ran while one was open for 23% -> 0% of each run, Pallas kernels for 0% -> 2%
where the time goes in v2:
time: 61.8 us; the launch traced here: 61.6 us
  starting transfers between devices  25.9 us (42%)
  waiting for transfers between devices  23.8 us (39%)
  Pallas kernels  8.47 us (14%)
  local copies, waits for them, and re-layouts  2.58 us (4%)
  between operations  0.8 us (1%)
    ppermute x16, waiting for transfers between devices, swap(): return lax.ppermute(value, axis, [(0, 1), (1, 0)])  15.4 us
    ppermute x8, starting transfers between devices, meet(): return lax.ppermute(value, AXES, pairs)  14.5 us
    ppermute x16, starting transfers between devices, swap(): return lax.ppermute(value, axis, [(0, 1), (1, 0)])  11.4 us
    pallas_call x18, Pallas kernels, run(): pl.pallas_call(kernel, out_shape=shapes, in_specs=in_specs or [VMEM] * le...  8.47 us
    ppermute x8, waiting for transfers between devices, meet(): return lax.ppermute(value, AXES, pairs)  8.36 us
    unnamed x14, local copies, waits for them, and re-layouts  2.58 us
  transfers between devices with their start and end apart: 24, of which 16 were waited for; matrix products, arithmetic and copies ran while one was open for 0% of the time, Pallas kernels for 2%

profile of v2, /device:TPU:0, one launch (start us, length us, event | category | flops | bytes accessed | tf_op | source)
XLA Modules:
  0.0 61.6 jit_solution(9444173808689537181)
XLA Ops:
  0.7 1.2 %copy-done.1 = bf16[1,160,16,128]{3,2,1,0:T(8,128)(2,1)S(1)} copy-done((bf16[1,160,16,128]{3,2,1,0:T(8,128)(2,1)S(1)}, bf16[1,160,16,128]{3,2,1,0:T(8,128)(2,1)}, u32[]{:S(2)}) %copy-start.1) | copy-done | bytes 655384
  3.2 1.4 %scale.1 = (bf16[3,2,160,128]{3,2,1,0:T(8,128)(2,1)S(1)}, bf16[3,2,160,128]{3,2,1,0:T(8,128)(2,1)S(1)}, bf16[1,2,160,128]{3,2,1,0:T(8,128)(2,1)S(1)}, bf16[1,2,160,128]{3,2,1,0:T(8,128)(2,1)S(1)}) custom-call(s32[16]{0:T(128)S(1)} %copy-done.4, bf16[160,16,128]{2,1,0:T(8,128)(2,1)S(1)} %bitcast.5, f32[1,160]{1,0:T(1,128)S(1)} %bitcast.6), custom_call_target="tpu_custom_call" | custom-call | bytes 1311424 | tf_op jit(solution)/shard_map/scale/pallas_call | solution.py:126
  5.2 1.2 %collective-permute-done.got = bf16[1,2,160,128]{3,2,1,0:T(8,128)(2,1)S(1)} collective-permute-done((bf16[1,2,160,128]{3,2,1,0:T(8,128)(2,1)S(1)}, bf16[1,2,160,128]{3,2,1,0:T(8,128)(2,1)S(1)}, u32[]{:S(2)}, u32[]{:S(2)}) %collective-permute-start) | collective-permute-done | bytes 81952 | tf_op jit(solution)/shard_map/ppermute | solution.py:42
  6.8 5.7 %collective-permute-start.1 = (bf16[2,2,160,128]{3,2,1,0:T(8,128)(2,1)S(1)}, bf16[2,2,160,128]{3,2,1,0:T(8,128)(2,1)S(1)}, u32[]{:S(2)}, u32[]{:S(2)}) collective-permute-start(bf16[2,2,160,128]{3,2,1,0:T(8,128)(2,1)S(1)} %join.4), channel_id=1, source_target_pairs={{0,28},{1,25},{2,30},{3,27},{4,24},{5,29},{6,26},{7,31},{8,20},{9,... | collective-permute-start | bytes 491528 | tf_op jit(solution)/shard_map/ppermute | solution.py:55
  12.5 1.6 %collective-permute-start.4 = (bf16[2,2,160,128]{3,2,1,0:T(8,128)(2,1)S(1)}, bf16[2,2,160,128]{3,2,1,0:T(8,128)(2,1)S(1)}, u32[]{:S(2)}, u32[]{:S(2)}) collective-permute-start(bf16[2,2,160,128]{3,2,1,0:T(8,128)(2,1)S(1)} %get-tuple-element.37.own), channel_id=1, source_target_pairs={{0,2},{2,0},{1,3},{3,1},{4,6},{6,4},{5,7},{7,5},{8,10},{10,8},{9,1... | collective-permute-start | bytes 491528 | tf_op jit(solution)/shard_map/ppermute | solution.py:42
  14.7 1.5 %collective-permute-start.8 = (bf16[2,2,160,128]{3,2,1,0:T(8,128)(2,1)S(1)}, bf16[2,2,160,128]{3,2,1,0:T(8,128)(2,1)S(1)}, u32[]{:S(2)}, u32[]{:S(2)}) collective-permute-start(bf16[2,2,160,128]{3,2,1,0:T(8,128)(2,1)S(1)} %get-tuple-element.39.own), channel_id=1, source_target_pairs={{0,2},{2,0},{1,3},{3,1},{4,6},{6,4},{5,7},{7,5},{8,10},{10,8},{9,1... | collective-permute-start | bytes 491528 | tf_op jit(solution)/shard_map/ppermute | solution.py:42
  16.2 1.2 %collective-permute-done.1.own = bf16[2,2,160,128]{3,2,1,0:T(8,128)(2,1)S(1)} collective-permute-done((bf16[2,2,160,128]{3,2,1,0:T(8,128)(2,1)S(1)}, bf16[2,2,160,128]{3,2,1,0:T(8,128)(2,1)S(1)}, u32[]{:S(2)}, u32[]{:S(2)}) %collective-permute-start.1) | collective-permute-done | bytes 163872 | tf_op jit(solution)/shard_map/ppermute | solution.py:55
  17.3 1.5 %collective-permute-start.2 = (bf16[2,2,160,128]{3,2,1,0:T(8,128)(2,1)S(1)}, bf16[2,2,160,128]{3,2,1,0:T(8,128)(2,1)S(1)}, u32[]{:S(2)}, u32[]{:S(2)}) collective-permute-start(bf16[2,2,160,128]{3,2,1,0:T(8,128)(2,1)S(1)} %collective-permute-done.1.own), channel_id=1, source_target_pairs={{0,2},{2,0},{1,3},{3,1},{4,6},{6,4},{5,7},{7,5},{8,10},{10,8},{9,1... | collective-permute-start | bytes 491528 | tf_op jit(solution)/shard_map/ppermute | solution.py:42
  19.8 3.3 %collective-permute-start.5 = (bf16[2,2,160,128]{3,2,1,0:T(8,128)(2,1)S(1)}, bf16[2,2,160,128]{3,2,1,0:T(8,128)(2,1)S(1)}, u32[]{:S(2)}, u32[]{:S(2)}) collective-permute-start(bf16[2,2,160,128]{3,2,1,0:T(8,128)(2,1)S(1)} %fold.9), channel_id=1, source_target_pairs={{0,16},{1,21},{2,18},{3,23},{4,20},{5,17},{6,22},{7,19},{8,24},{9,... | collective-permute-start | bytes 491528 | tf_op jit(solution)/shard_map/ppermute | solution.py:55
  23.4 3.2 %collective-permute-done.8.peer = bf16[2,2,160,128]{3,2,1,0:T(8,128)(2,1)S(1)} collective-permute-done((bf16[2,2,160,128]{3,2,1,0:T(8,128)(2,1)S(1)}, bf16[2,2,160,128]{3,2,1,0:T(8,128)(2,1)S(1)}, u32[]{:S(2)}, u32[]{:S(2)}) %collective-permute-start.8) | collective-permute-done | bytes 163872 | tf_op jit(solution)/shard_map/ppermute | solution.py:42
  28.5 1.2 %collective-permute-done.5.refs_1_ = bf16[2,2,160,128]{3,2,1,0:T(8,128)(2,1)S(1)} collective-permute-done((bf16[2,2,160,128]{3,2,1,0:T(8,128)(2,1)S(1)}, bf16[2,2,160,128]{3,2,1,0:T(8,128)(2,1)S(1)}, u32[]{:S(2)}, u32[]{:S(2)}) %collective-permute-start.5) | collective-permute-done | bytes 163872 | tf_op jit(solution)/shard_map/ppermute | solution.py:55
  30.1 1.5 %collective-permute-start.11 = (bf16[4,2,160,128]{3,2,1,0:T(8,128)(2,1)S(1)}, bf16[4,2,160,128]{3,2,1,0:T(8,128)(2,1)S(1)}, u32[]{:S(2)}, u32[]{:S(2)}) collective-permute-start(bf16[4,2,160,128]{3,2,1,0:T(8,128)(2,1)S(1)} %get-tuple-element.43), channel_id=1, source_target_pairs={{0,1},{1,0},{2,3},{3,2},{4,5},{5,4},{6,7},{7,6},{8,9},{9,8},{10,11... | collective-permute-start | bytes 983048 | tf_op jit(solution)/shard_map/ppermute | solution.py:42
  32.9 4.1 %solve.1 = (bf16[640,256]{1,0:T(8,128)(2,1)S(1)}, bf16[640,256]{1,0:T(8,128)(2,1)S(1)}, bf16[3,2,160,128]{3,2,1,0:T(8,128)(2,1)S(1)}, bf16[3,2,160,128]{3,2,1,0:...) custom-call(s32[16]{0:T(128)S(1)} %copy-done.4, ...), custom_call_target="tpu_custom_call" | custom-call | bytes 9307200 | tf_op jit(solution)/shard_map/solve/pallas_call | solution.py:126
  37.5 1.1 %collective-permute-done.12.got = bf16[1,2,160,128]{3,2,1,0:T(8,128)(2,1)S(1)} collective-permute-done((bf16[1,2,160,128]{3,2,1,0:T(8,128)(2,1)S(1)}, bf16[1,2,160,128]{3,2,1,0:T(8,128)(2,1)S(1)}, u32[]{:S(2)}, u32[]{:S(2)}) %collective-permute-start.12) | collective-permute-done | bytes 81952 | tf_op jit(solution)/shard_map/ppermute | solution.py:42
  38.7 2.0 %collective-permute-start.13 = (bf16[2,2,160,128]{3,2,1,0:T(8,128)(2,1)S(1)}, bf16[2,2,160,128]{3,2,1,0:T(8,128)(2,1)S(1)}, u32[]{:S(2)}, u32[]{:S(2)}) collective-permute-start(bf16[2,2,160,128]{3,2,1,0:T(8,128)(2,1)S(1)} %join.6), channel_id=1, source_target_pairs={{0,28},{1,25},{2,30},{3,27},{4,24},{5,29},{6,26},{7,31},{8,20},{9,... | collective-permute-start | bytes 491528 | tf_op jit(solution)/shard_map/ppermute | solution.py:55
  41.3 1.5 %collective-permute-start.18 = (bf16[2,2,160,128]{3,2,1,0:T(8,128)(2,1)S(1)}, bf16[2,2,160,128]{3,2,1,0:T(8,128)(2,1)S(1)}, u32[]{:S(2)}, u32[]{:S(2)}) collective-permute-start(bf16[2,2,160,128]{3,2,1,0:T(8,128)(2,1)S(1)} %get-tuple-element.53.own), channel_id=1, source_target_pairs={{0,2},{2,0},{1,3},{3,1},{4,6},{6,4},{5,7},{7,5},{8,10},{10,8},{9,1... | collective-permute-start | bytes 491528 | tf_op jit(solution)/shard_map/ppermute | solution.py:42
  43.3 4.5 %collective-permute-done.13.own = bf16[2,2,160,128]{3,2,1,0:T(8,128)(2,1)S(1)} collective-permute-done((bf16[2,2,160,128]{3,2,1,0:T(8,128)(2,1)S(1)}, bf16[2,2,160,128]{3,2,1,0:T(8,128)(2,1)S(1)}, u32[]{:S(2)}, u32[]{:S(2)}) %collective-permute-start.13) | collective-permute-done | bytes 163872 | tf_op jit(solution)/shard_map/ppermute | solution.py:55
  48.4 2.0 %collective-permute-start.17 = (bf16[2,2,160,128]{3,2,1,0:T(8,128)(2,1)S(1)}, bf16[2,2,160,128]{3,2,1,0:T(8,128)(2,1)S(1)}, u32[]{:S(2)}, u32[]{:S(2)}) collective-permute-start(bf16[2,2,160,128]{3,2,1,0:T(8,128)(2,1)S(1)} %fold.13), channel_id=1, source_target_pairs={{0,16},{1,21},{2,18},{3,23},{4,20},{5,17},{6,22},{7,19},{8,24},{9,... | collective-permute-start | bytes 491528 | tf_op jit(solution)/shard_map/ppermute | solution.py:55
  50.4 1.0 %collective-permute-done.18.peer = bf16[2,2,160,128]{3,2,1,0:T(8,128)(2,1)S(1)} collective-permute-done((bf16[2,2,160,128]{3,2,1,0:T(8,128)(2,1)S(1)}, bf16[2,2,160,128]{3,2,1,0:T(8,128)(2,1)S(1)}, u32[]{:S(2)}, u32[]{:S(2)}) %collective-permute-start.18) | collective-permute-done | bytes 163872 | tf_op jit(solution)/shard_map/ppermute | solution.py:42
  51.6 3.4 %collective-permute-done.20.peer = bf16[2,2,160,128]{3,2,1,0:T(8,128)(2,1)S(1)} collective-permute-done((bf16[2,2,160,128]{3,2,1,0:T(8,128)(2,1)S(1)}, bf16[2,2,160,128]{3,2,1,0:T(8,128)(2,1)S(1)}, u32[]{:S(2)}, u32[]{:S(2)}) %collective-permute-start.20) | collective-permute-done | bytes 163872 | tf_op jit(solution)/shard_map/ppermute | solution.py:42
  55.7 1.2 %collective-permute-done.14.peer = bf16[2,2,160,128]{3,2,1,0:T(8,128)(2,1)S(1)} collective-permute-done((bf16[2,2,160,128]{3,2,1,0:T(8,128)(2,1)S(1)}, bf16[2,2,160,128]{3,2,1,0:T(8,128)(2,1)S(1)}, u32[]{:S(2)}, u32[]{:S(2)}) %collective-permute-start.14) | collective-permute-done | bytes 163872 | tf_op jit(solution)/shard_map/ppermute | solution.py:42
  57.0 1.1 %collective-permute-done.19.refs_2_ = bf16[2,2,160,128]{3,2,1,0:T(8,128)(2,1)S(1)} collective-permute-done((bf16[2,2,160,128]{3,2,1,0:T(8,128)(2,1)S(1)}, bf16[2,2,160,128]{3,2,1,0:T(8,128)(2,1)S(1)}, u32[]{:S(2)}, u32[]{:S(2)}) %collective-permute-start.19) | collective-permute-done | bytes 163872 | tf_op jit(solution)/shard_map/ppermute | solution.py:55
  58.3 1.5 %collective-permute-done.23.got = bf16[4,2,160,128]{3,2,1,0:T(8,128)(2,1)S(1)} collective-permute-done((bf16[4,2,160,128]{3,2,1,0:T(8,128)(2,1)S(1)}, bf16[4,2,160,128]{3,2,1,0:T(8,128)(2,1)S(1)}, u32[]{:S(2)}, u32[]{:S(2)}) %collective-permute-start.23) | collective-permute-done | bytes 327712 | tf_op jit(solution)/shard_map/ppermute | solution.py:42
  59.8 1.8 %place.1 = (bf16[160,16,128]{2,1,0:T(8,128)(2,1)}, bf16[640,512]{1,0:T(8,128)(2,1)}) custom-call(s32[16]{0:T(128)S(1)} %copy-done.4, bf16[4,2,160,128]{3,2,1,0:T(8,128)(2,1)S(1)} %get-tuple-element.58.keep, bf16[4,2,160,128]{3,2,1,0:T(8,128)(2,1)S(1)} %collective-permute-done.23.got, bf16[640,256]{1,0:T(8,128)(2,1)S(1)} %get-tuple-element.60.spec_mine, ...), custom_call_target="tpu_custom_call" | custom-call | bytes 2621504 | tf_op jit(solution)/shard_map/place/pallas_call | solution.py:126
  (56 shorter events, 11.1 us)
Async XLA Ops:
  4.6 1.8 %collective-permute-start.3 = (bf16[3,2,160,128]{3,2,1,0:T(8,128)(2,1)S(1)}, bf16[3,2,160,128]{3,2,1,0:T(8,128)(2,1)S(1)}, u32[]{:S(2)}, u32[]{:S(2)}) collective-permute-start(bf16[3,2,160,128]{3,2,1,0:T(8,128)(2,1)S(1)} %get-tuple-element.36), channel_id=1, source_target_pairs={{0,1},{1,0},{2,3},{3,2},{4,5},{5,4},{6,7},{7,6},{8,9},{9,8},{10,11... | collective-permute-start | bytes 737288 | tf_op jit(solution)/shard_map/ppermute | solution.py:42
  5.1 1.3 %collective-permute-start = (bf16[1,2,160,128]{3,2,1,0:T(8,128)(2,1)S(1)}, bf16[1,2,160,128]{3,2,1,0:T(8,128)(2,1)S(1)}, u32[]{:S(2)}, u32[]{:S(2)}) collective-permute-start(bf16[1,2,160,128]{3,2,1,0:T(8,128)(2,1)S(1)} %get-tuple-element.34), channel_id=1, source_target_pairs={{0,1},{1,0},{2,3},{3,2},{4,5},{5,4},{6,7},{7,6},{8,9},{9,8},{10,11... | collective-permute-start | bytes 245768 | tf_op jit(solution)/shard_map/ppermute | solution.py:42
  6.4 22.1 %collective-permute-start.10 = (bf16[2,1,640,1280]{3,2,1,0:T(8,128)(2,1)}, bf16[2,1,640,1280]{3,2,1,0:T(8,128)(2,1)S(1)}, u32[]{:S(2)}, u32[]{:S(2)}) collective-permute-start(bf16[2,1,640,1280]{3,2,1,0:T(8,128)(2,1)} %tables_mine.1), channel_id=1, source_target_pairs={{0,1},{1,0},{2,3},{3,2},{4,5},{5,4},{6,7},{7,6},{8,9},{9,8},{10,11... | collective-permute-start | bytes 9830408 | tf_op jit(solution)/shard_map/ppermute | solution.py:42
  6.8 10.6 %collective-permute-start.1 = (bf16[2,2,160,128]{3,2,1,0:T(8,128)(2,1)S(1)}, bf16[2,2,160,128]{3,2,1,0:T(8,128)(2,1)S(1)}, u32[]{:S(2)}, u32[]{:S(2)}) collective-permute-start(bf16[2,2,160,128]{3,2,1,0:T(8,128)(2,1)S(1)} %join.4), channel_id=1, source_target_pairs={{0,28},{1,25},{2,30},{3,27},{4,24},{5,29},{6,26},{7,31},{8,20},{9,... | collective-permute-start | bytes 491528 | tf_op jit(solution)/shard_map/ppermute | solution.py:55
  12.5 7.2 %collective-permute-start.4 = (bf16[2,2,160,128]{3,2,1,0:T(8,128)(2,1)S(1)}, bf16[2,2,160,128]{3,2,1,0:T(8,128)(2,1)S(1)}, u32[]{:S(2)}, u32[]{:S(2)}) collective-permute-start(bf16[2,2,160,128]{3,2,1,0:T(8,128)(2,1)S(1)} %get-tuple-element.37.own), channel_id=1, source_target_pairs={{0,2},{2,0},{1,3},{3,1},{4,6},{6,4},{5,7},{7,5},{8,10},{10,8},{9,1... | collective-permute-start | bytes 491528 | tf_op jit(solution)/shard_map/ppermute | solution.py:42
  14.1 9.2 %collective-permute-start.6 = (bf16[2,2,160,128]{3,2,1,0:T(8,128)(2,1)S(1)}, bf16[2,2,160,128]{3,2,1,0:T(8,128)(2,1)S(1)}, u32[]{:S(2)}, u32[]{:S(2)}) collective-permute-start(bf16[2,2,160,128]{3,2,1,0:T(8,128)(2,1)S(1)} %get-tuple-element.38.own), channel_id=1, source_target_pairs={{0,2},{2,0},{1,3},{3,1},{4,6},{6,4},{5,7},{7,5},{8,10},{10,8},{9,1... | collective-permute-start | bytes 491528 | tf_op jit(solution)/shard_map/ppermute | solution.py:42
  14.7 12.0 %collective-permute-start.8 = (bf16[2,2,160,128]{3,2,1,0:T(8,128)(2,1)S(1)}, bf16[2,2,160,128]{3,2,1,0:T(8,128)(2,1)S(1)}, u32[]{:S(2)}, u32[]{:S(2)}) collective-permute-start(bf16[2,2,160,128]{3,2,1,0:T(8,128)(2,1)S(1)} %get-tuple-element.39.own), channel_id=1, source_target_pairs={{0,2},{2,0},{1,3},{3,1},{4,6},{6,4},{5,7},{7,5},{8,10},{10,8},{9,1... | collective-permute-start | bytes 491528 | tf_op jit(solution)/shard_map/ppermute | solution.py:42
  17.3 11.1 %collective-permute-start.2 = (bf16[2,2,160,128]{3,2,1,0:T(8,128)(2,1)S(1)}, bf16[2,2,160,128]{3,2,1,0:T(8,128)(2,1)S(1)}, u32[]{:S(2)}, u32[]{:S(2)}) collective-permute-start(bf16[2,2,160,128]{3,2,1,0:T(8,128)(2,1)S(1)} %collective-permute-done.1.own), channel_id=1, source_target_pairs={{0,2},{2,0},{1,3},{3,1},{4,6},{6,4},{5,7},{7,5},{8,10},{10,8},{9,1... | collective-permute-start | bytes 491528 | tf_op jit(solution)/shard_map/ppermute | solution.py:42
  19.8 9.9 %collective-permute-start.5 = (bf16[2,2,160,128]{3,2,1,0:T(8,128)(2,1)S(1)}, bf16[2,2,160,128]{3,2,1,0:T(8,128)(2,1)S(1)}, u32[]{:S(2)}, u32[]{:S(2)}) collective-permute-start(bf16[2,2,160,128]{3,2,1,0:T(8,128)(2,1)S(1)} %fold.9), channel_id=1, source_target_pairs={{0,16},{1,21},{2,18},{3,23},{4,20},{5,17},{6,22},{7,19},{8,24},{9,... | collective-permute-start | bytes 491528 | tf_op jit(solution)/shard_map/ppermute | solution.py:55
  23.3 6.7 %collective-permute-start.7 = (bf16[2,2,160,128]{3,2,1,0:T(8,128)(2,1)S(1)}, bf16[2,2,160,128]{3,2,1,0:T(8,128)(2,1)S(1)}, u32[]{:S(2)}, u32[]{:S(2)}) collective-permute-start(bf16[2,2,160,128]{3,2,1,0:T(8,128)(2,1)S(1)} %fold.10), channel_id=1, source_target_pairs={{0,8},{1,13},{2,10},{3,15},{4,12},{5,9},{6,14},{7,11},{8,0},{9,5},... | collective-permute-start | bytes 491528 | tf_op jit(solution)/shard_map/ppermute | solution.py:55
  26.7 3.4 %collective-permute-start.9 = (bf16[2,2,160,128]{3,2,1,0:T(8,128)(2,1)S(1)}, bf16[2,2,160,128]{3,2,1,0:T(8,128)(2,1)S(1)}, u32[]{:S(2)}, u32[]{:S(2)}) collective-permute-start(bf16[2,2,160,128]{3,2,1,0:T(8,128)(2,1)S(1)} %fold.11.refs_4_), channel_id=1, source_target_pairs={{1,5},{3,7},{5,1},{7,3},{9,13},{11,15},{13,9},{15,11},{17,21},{19,... | collective-permute-start | bytes 491528 | tf_op jit(solution)/shard_map/ppermute | solution.py:55
  30.1 2.7 %collective-permute-start.11 = (bf16[4,2,160,128]{3,2,1,0:T(8,128)(2,1)S(1)}, bf16[4,2,160,128]{3,2,1,0:T(8,128)(2,1)S(1)}, u32[]{:S(2)}, u32[]{:S(2)}) collective-permute-start(bf16[4,2,160,128]{3,2,1,0:T(8,128)(2,1)S(1)} %get-tuple-element.43), channel_id=1, source_target_pairs={{0,1},{1,0},{2,3},{3,2},{4,5},{5,4},{6,7},{7,6},{8,9},{9,8},{10,11... | collective-permute-start | bytes 983048 | tf_op jit(solution)/shard_map/ppermute | solution.py:42
  37.0 3.7 %collective-permute-start.15 = (bf16[3,2,160,128]{3,2,1,0:T(8,128)(2,1)S(1)}, bf16[3,2,160,128]{3,2,1,0:T(8,128)(2,1)S(1)}, u32[]{:S(2)}, u32[]{:S(2)}) collective-permute-start(bf16[3,2,160,128]{3,2,1,0:T(8,128)(2,1)S(1)} %get-tuple-element.51), channel_id=1, source_target_pairs={{0,1},{1,0},{2,3},{3,2},{4,5},{5,4},{6,7},{7,6},{8,9},{9,8},{10,11... | collective-permute-start | bytes 737288 | tf_op jit(solution)/shard_map/ppermute | solution.py:42
  37.4 1.3 %collective-permute-start.12 = (bf16[1,2,160,128]{3,2,1,0:T(8,128)(2,1)S(1)}, bf16[1,2,160,128]{3,2,1,0:T(8,128)(2,1)S(1)}, u32[]{:S(2)}, u32[]{:S(2)}) collective-permute-start(bf16[1,2,160,128]{3,2,1,0:T(8,128)(2,1)S(1)} %get-tuple-element.49), channel_id=1, source_target_pairs={{0,1},{1,0},{2,3},{3,2},{4,5},{5,4},{6,7},{7,6},{8,9},{9,8},{10,11... | collective-permute-start | bytes 245768 | tf_op jit(solution)/shard_map/ppermute | solution.py:42
  38.7 9.2 %collective-permute-start.13 = (bf16[2,2,160,128]{3,2,1,0:T(8,128)(2,1)S(1)}, bf16[2,2,160,128]{3,2,1,0:T(8,128)(2,1)S(1)}, u32[]{:S(2)}, u32[]{:S(2)}) collective-permute-start(bf16[2,2,160,128]{3,2,1,0:T(8,128)(2,1)S(1)} %join.6), channel_id=1, source_target_pairs={{0,28},{1,25},{2,30},{3,27},{4,24},{5,29},{6,26},{7,31},{8,20},{9,... | collective-permute-start | bytes 491528 | tf_op jit(solution)/shard_map/ppermute | solution.py:55
  40.7 7.6 %collective-permute-start.16 = (bf16[2,2,160,128]{3,2,1,0:T(8,128)(2,1)S(1)}, bf16[2,2,160,128]{3,2,1,0:T(8,128)(2,1)S(1)}, u32[]{:S(2)}, u32[]{:S(2)}) collective-permute-start(bf16[2,2,160,128]{3,2,1,0:T(8,128)(2,1)S(1)} %get-tuple-element.52.own), channel_id=1, source_target_pairs={{0,2},{2,0},{1,3},{3,1},{4,6},{6,4},{5,7},{7,5},{8,10},{10,8},{9,1... | collective-permute-start | bytes 491528 | tf_op jit(solution)/shard_map/ppermute | solution.py:42
  41.3 10.1 %collective-permute-start.18 = (bf16[2,2,160,128]{3,2,1,0:T(8,128)(2,1)S(1)}, bf16[2,2,160,128]{3,2,1,0:T(8,128)(2,1)S(1)}, u32[]{:S(2)}, u32[]{:S(2)}) collective-permute-start(bf16[2,2,160,128]{3,2,1,0:T(8,128)(2,1)S(1)} %get-tuple-element.53.own), channel_id=1, source_target_pairs={{0,2},{2,0},{1,3},{3,1},{4,6},{6,4},{5,7},{7,5},{8,10},{10,8},{9,1... | collective-permute-start | bytes 491528 | tf_op jit(solution)/shard_map/ppermute | solution.py:42
  42.8 14.1 %collective-permute-start.22 = (bf16[640,256]{1,0:T(8,128)(2,1)S(1)}, bf16[640,256]{1,0:T(8,128)(2,1)S(1)}, u32[]{:S(2)}, u32[]{:S(2)}) collective-permute-start(bf16[640,256]{1,0:T(8,128)(2,1)S(1)} %get-tuple-element.56), channel_id=1, source_target_pairs={{0,1},{1,0},{2,3},{3,2},{4,5},{5,4},{6,7},{7,6},{8,9},{9,8},{10,11... | collective-permute-start | bytes 983048 | tf_op jit(solution)/shard_map/ppermute | solution.py:42
  42.8 12.1 %collective-permute-start.20 = (bf16[2,2,160,128]{3,2,1,0:T(8,128)(2,1)S(1)}, bf16[2,2,160,128]{3,2,1,0:T(8,128)(2,1)S(1)}, u32[]{:S(2)}, u32[]{:S(2)}) collective-permute-start(bf16[2,2,160,128]{3,2,1,0:T(8,128)(2,1)S(1)} %get-tuple-element.54.own), channel_id=1, source_target_pairs={{0,2},{2,0},{1,3},{3,1},{4,6},{6,4},{5,7},{7,5},{8,10},{10,8},{9,1... | collective-permute-start | bytes 491528 | tf_op jit(solution)/shard_map/ppermute | solution.py:42
  47.9 9.0 %collective-permute-start.14 = (bf16[2,2,160,128]{3,2,1,0:T(8,128)(2,1)S(1)}, bf16[2,2,160,128]{3,2,1,0:T(8,128)(2,1)S(1)}, u32[]{:S(2)}, u32[]{:S(2)}) collective-permute-start(bf16[2,2,160,128]{3,2,1,0:T(8,128)(2,1)S(1)} %collective-permute-done.13.own), channel_id=1, source_target_pairs={{0,2},{2,0},{1,3},{3,1},{4,6},{6,4},{5,7},{7,5},{8,10},{10,8},{9,1... | collective-permute-start | bytes 491528 | tf_op jit(solution)/shard_map/ppermute | solution.py:42
  48.4 8.5 %collective-permute-start.17 = (bf16[2,2,160,128]{3,2,1,0:T(8,128)(2,1)S(1)}, bf16[2,2,160,128]{3,2,1,0:T(8,128)(2,1)S(1)}, u32[]{:S(2)}, u32[]{:S(2)}) collective-permute-start(bf16[2,2,160,128]{3,2,1,0:T(8,128)(2,1)S(1)} %fold.13), channel_id=1, source_target_pairs={{0,16},{1,21},{2,18},{3,23},{4,20},{5,17},{6,22},{7,19},{8,24},{9,... | collective-permute-start | bytes 491528 | tf_op jit(solution)/shard_map/ppermute | solution.py:55
  51.5 6.5 %collective-permute-start.19 = (bf16[2,2,160,128]{3,2,1,0:T(8,128)(2,1)S(1)}, bf16[2,2,160,128]{3,2,1,0:T(8,128)(2,1)S(1)}, u32[]{:S(2)}, u32[]{:S(2)}) collective-permute-start(bf16[2,2,160,128]{3,2,1,0:T(8,128)(2,1)S(1)} %fold.14), channel_id=1, source_target_pairs={{0,8},{1,13},{2,10},{3,15},{4,12},{5,9},{6,14},{7,11},{8,0},{9,5},... | collective-permute-start | bytes 491528 | tf_op jit(solution)/shard_map/ppermute | solution.py:55
  55.0 3.0 %collective-permute-start.21 = (bf16[2,2,160,128]{3,2,1,0:T(8,128)(2,1)S(1)}, bf16[2,2,160,128]{3,2,1,0:T(8,128)(2,1)S(1)}, u32[]{:S(2)}, u32[]{:S(2)}) collective-permute-start(bf16[2,2,160,128]{3,2,1,0:T(8,128)(2,1)S(1)} %fold.15.refs_4_), channel_id=1, source_target_pairs={{1,5},{3,7},{5,1},{7,3},{9,13},{11,15},{13,9},{15,11},{17,21},{19,... | collective-permute-start | bytes 491528 | tf_op jit(solution)/shard_map/ppermute | solution.py:55
  58.1 1.7 %collective-permute-start.23 = (bf16[4,2,160,128]{3,2,1,0:T(8,128)(2,1)S(1)}, bf16[4,2,160,128]{3,2,1,0:T(8,128)(2,1)S(1)}, u32[]{:S(2)}, u32[]{:S(2)}) collective-permute-start(bf16[4,2,160,128]{3,2,1,0:T(8,128)(2,1)S(1)} %get-tuple-element.59), channel_id=1, source_target_pairs={{0,1},{1,0},{2,3},{3,2},{4,5},{5,4},{6,7},{7,6},{8,9},{9,8},{10,11... | collective-permute-start | bytes 983048 | tf_op jit(solution)/shard_map/ppermute | solution.py:42
  (7 other events, 120.0 us)

commit v3 on v2

--- a/solution.py
+++ b/solution.py
@@ -26,16 +26,18 @@
     )
 
 
-RAW_STEPS = 1
-
-
 def mask_plan(owners):
-    even = range(owners - 2, -1, -2)
-    cores = [
-        [mask + (1 - core if step < RAW_STEPS else core) for step, mask in enumerate(even)]
-        for core in range(2)
-    ]
-    return [masks[RAW_STEPS:] for masks in cores], [masks[:RAW_STEPS] for masks in cores]
+    middle = owners // 2
+    fold, raw = [], []
+    for core in range(2):
+        far = [
+            even + (i + 1 + core) % 2 for i, even in enumerate(range(owners - 2, middle - 1, -2))
+        ]
+        first = core * middle // 2
+        near = list(range(first + middle // 2 - 1, first - 1, -1))
+        raw.append(far[0::2] + near[0::2])
+        fold.append(far[1::2] + near[1::2])
+    return fold, raw
 
 
 def swap(value, axis):
@@ -107,11 +109,13 @@
     fold_got = swap(fold_other, "lev")
     raw_sent = call(join_kernel, (block,) * raws, "join", 8)(raw_mine, raw_got)
     raw = [meet(b, (raw_masks[0][i], raw_masks[1][i])) for i, b in enumerate(raw_sent)]
-    raw_folded = [fold(b, swap(b, "parity")) for b in raw]
+    raw_peer = [swap(b, "parity") for b in raw]
     aside = aside((fold_got, raw_got))
     plain = call(join_kernel, (block,) * folds, "join", 8)(fold_mine, fold_got)
     sent = [fold(b, swap(b, "parity")) for b in plain]
     folded = [meet(b, (fold_masks[0][i], fold_masks[1][i])) for i, b in enumerate(sent)]
+    raw_peer[0] = lax.optimization_barrier((raw_peer[0], folded[0]))[0]
+    raw_folded = [fold(b, peer) for b, peer in zip(raw, raw_peer)]
     last, aside = lax.optimization_barrier((sent[-1], aside))
     whole = jax.ShapeDtypeStruct((folds + raws, 2, rows, side), jnp.bfloat16)
     keep, give = call(

time: 61.8 us -> 60.2 us (0.974)
  waiting for transfers between devices: 23.8 us -> 19.3 us
  starting transfers between devices: 25.9 us -> 28.9 us
    ppermute x16, waiting for transfers between devices: 15.4 us -> 7.76 us  [swap(): return lax.ppermute(value, axis, [(0, 1), (1, 0)])]
    ppermute x8, starting transfers between devices: 14.5 us -> 18.2 us  [meet(): return lax.ppermute(value, AXES, pairs)]
    ppermute x8, waiting for transfers between devices: 8.36 us -> 11.5 us  [meet(): return lax.ppermute(value, AXES, pairs)]
    ppermute x16, starting transfers between devices: 11.4 us -> 10.7 us  [swap(): return lax.ppermute(value, axis, [(0, 1), (1, 0)])]
  transfers between devices with their start and end apart: 24 -> 24, of which waited for: 16 -> 12; matrix products, arithmetic and copies ran while one was open for 0% -> 0% of each run, Pallas kernels for 2% -> 2%
where the time goes in v3:
time: 60.2 us; the launch traced here: 60 us
  starting transfers between devices  28.9 us (48%)
  waiting for transfers between devices  19.3 us (32%)
  Pallas kernels  8.48 us (14%)
  local copies, waits for them, and re-layouts  2.58 us (4%)
  between operations  0.82 us (1%)
    ppermute x8, starting transfers between devices, meet(): return lax.ppermute(value, AXES, pairs)  18.2 us
    ppermute x8, waiting for transfers between devices, meet(): return lax.ppermute(value, AXES, pairs)  11.5 us
    ppermute x16, starting transfers between devices, swap(): return lax.ppermute(value, axis, [(0, 1), (1, 0)])  10.7 us
    pallas_call x18, Pallas kernels, run(): pl.pallas_call(kernel, out_shape=shapes, in_specs=in_specs or [VMEM] * le...  8.48 us
    ppermute x16, waiting for transfers between devices, swap(): return lax.ppermute(value, axis, [(0, 1), (1, 0)])  7.76 us
    unnamed x14, local copies, waits for them, and re-layouts  2.58 us
  transfers between devices with their start and end apart: 24, of which 12 were waited for; matrix products, arithmetic and copies ran while one was open for 0% of the time, Pallas kernels for 2%

profile of v3, /device:TPU:0, one launch (start us, length us, event | category | flops | bytes accessed | tf_op | source)
XLA Modules:
  0.0 60.0 jit_solution(1956301131225062817)
XLA Ops:
  0.7 1.2 %copy-done.1 = bf16[1,160,16,128]{3,2,1,0:T(8,128)(2,1)S(1)} copy-done((bf16[1,160,16,128]{3,2,1,0:T(8,128)(2,1)S(1)}, bf16[1,160,16,128]{3,2,1,0:T(8,128)(2,1)}, u32[]{:S(2)}) %copy-start.1) | copy-done | bytes 655384
  3.2 1.4 %scale.1 = (bf16[2,2,160,128]{3,2,1,0:T(8,128)(2,1)S(1)}, bf16[2,2,160,128]{3,2,1,0:T(8,128)(2,1)S(1)}, bf16[2,2,160,128]{3,2,1,0:T(8,128)(2,1)S(1)}, bf16[2,2,160,128]{3,2,1,0:T(8,128)(2,1)S(1)}) custom-call(s32[16]{0:T(128)S(1)} %copy-done.4, bf16[160,16,128]{2,1,0:T(8,128)(2,1)S(1)} %bitcast.5, f32[1,160]{1,0:T(1,128)S(1)} %bitcast.6), custom_call_target="tpu_custom_call" | custom-call | bytes 1311424 | tf_op jit(solution)/shard_map/scale/pallas_call | solution.py:130
  5.2 0.9 %collective-permute-done.got = bf16[2,2,160,128]{3,2,1,0:T(8,128)(2,1)S(1)} collective-permute-done((bf16[2,2,160,128]{3,2,1,0:T(8,128)(2,1)S(1)}, bf16[2,2,160,128]{3,2,1,0:T(8,128)(2,1)S(1)}, u32[]{:S(2)}, u32[]{:S(2)}) %collective-permute-start) | collective-permute-done | bytes 163872 | tf_op jit(solution)/shard_map/ppermute | solution.py:44
  6.8 5.9 %collective-permute-start.1 = (bf16[2,2,160,128]{3,2,1,0:T(8,128)(2,1)S(1)}, bf16[2,2,160,128]{3,2,1,0:T(8,128)(2,1)S(1)}, u32[]{:S(2)}, u32[]{:S(2)}) collective-permute-start(bf16[2,2,160,128]{3,2,1,0:T(8,128)(2,1)S(1)} %get-tuple-element.39), channel_id=1, source_target_pairs={{0,28},{1,25},{2,30},{3,27},{4,24},{5,29},{6,26},{7,31},{8,20},{9,... | collective-permute-start | bytes 491528 | tf_op jit(solution)/shard_map/ppermute | solution.py:57
  12.7 1.6 %collective-permute-start.4 = (bf16[2,2,160,128]{3,2,1,0:T(8,128)(2,1)S(1)}, bf16[2,2,160,128]{3,2,1,0:T(8,128)(2,1)S(1)}, u32[]{:S(2)}, u32[]{:S(2)}) collective-permute-start(bf16[2,2,160,128]{3,2,1,0:T(8,128)(2,1)S(1)} %get-tuple-element.42.own), channel_id=1, source_target_pairs={{0,2},{2,0},{1,3},{3,1},{4,6},{6,4},{5,7},{7,5},{8,10},{10,8},{9,1... | collective-permute-start | bytes 491528 | tf_op jit(solution)/shard_map/ppermute | solution.py:44
  15.3 2.4 %collective-permute-done.1.own = bf16[2,2,160,128]{3,2,1,0:T(8,128)(2,1)S(1)} collective-permute-done((bf16[2,2,160,128]{3,2,1,0:T(8,128)(2,1)S(1)}, bf16[2,2,160,128]{3,2,1,0:T(8,128)(2,1)S(1)}, u32[]{:S(2)}, u32[]{:S(2)}) %collective-permute-start.1) | collective-permute-done | bytes 163872 | tf_op jit(solution)/shard_map/ppermute | solution.py:57
  17.7 1.8 %collective-permute-start.2 = (bf16[2,2,160,128]{3,2,1,0:T(8,128)(2,1)S(1)}, bf16[2,2,160,128]{3,2,1,0:T(8,128)(2,1)S(1)}, u32[]{:S(2)}, u32[]{:S(2)}) collective-permute-start(bf16[2,2,160,128]{3,2,1,0:T(8,128)(2,1)S(1)} %collective-permute-done.1.own), channel_id=1, source_target_pairs={{0,2},{2,0},{1,3},{3,1},{4,6},{6,4},{5,7},{7,5},{8,10},{10,8},{9,1... | collective-permute-start | bytes 491528 | tf_op jit(solution)/shard_map/ppermute | solution.py:44
  19.9 3.2 %collective-permute-start.5 = (bf16[2,2,160,128]{3,2,1,0:T(8,128)(2,1)S(1)}, bf16[2,2,160,128]{3,2,1,0:T(8,128)(2,1)S(1)}, u32[]{:S(2)}, u32[]{:S(2)}) collective-permute-start(bf16[2,2,160,128]{3,2,1,0:T(8,128)(2,1)S(1)} %fold.8), channel_id=1, source_target_pairs={{0,16},{1,21},{2,18},{3,23},{4,20},{5,17},{6,22},{7,19},{8,24},{9,... | collective-permute-start | bytes 491528 | tf_op jit(solution)/shard_map/ppermute | solution.py:57
  24.4 0.7 %collective-permute-done.2.peer = bf16[2,2,160,128]{3,2,1,0:T(8,128)(2,1)S(1)} collective-permute-done((bf16[2,2,160,128]{3,2,1,0:T(8,128)(2,1)S(1)}, bf16[2,2,160,128]{3,2,1,0:T(8,128)(2,1)S(1)}, u32[]{:S(2)}, u32[]{:S(2)}) %collective-permute-start.2) | collective-permute-done | bytes 163872 | tf_op jit(solution)/shard_map/ppermute | solution.py:44
  25.1 3.6 %collective-permute-done.5.refs_2_ = bf16[2,2,160,128]{3,2,1,0:T(8,128)(2,1)S(1)} collective-permute-done((bf16[2,2,160,128]{3,2,1,0:T(8,128)(2,1)S(1)}, bf16[2,2,160,128]{3,2,1,0:T(8,128)(2,1)S(1)}, u32[]{:S(2)}, u32[]{:S(2)}) %collective-permute-start.5) | collective-permute-done | bytes 163872 | tf_op jit(solution)/shard_map/ppermute | solution.py:57
  30.0 0.7 %collective-permute-done.11.got = bf16[4,2,160,128]{3,2,1,0:T(8,128)(2,1)S(1)} collective-permute-done((bf16[4,2,160,128]{3,2,1,0:T(8,128)(2,1)S(1)}, bf16[4,2,160,128]{3,2,1,0:T(8,128)(2,1)S(1)}, u32[]{:S(2)}, u32[]{:S(2)}) %collective-permute-start.11) | collective-permute-done | bytes 327712 | tf_op jit(solution)/shard_map/ppermute | solution.py:44
  30.7 4.1 %solve.1 = (bf16[640,256]{1,0:T(8,128)(2,1)S(1)}, bf16[640,256]{1,0:T(8,128)(2,1)S(1)}, bf16[2,2,160,128]{3,2,1,0:T(8,128)(2,1)S(1)}, bf16[2,2,160,128]{3,2,1,0:...) custom-call(s32[16]{0:T(128)S(1)} %copy-done.4, ...), custom_call_target="tpu_custom_call" | custom-call | bytes 9307200 | tf_op jit(solution)/shard_map/solve/pallas_call | solution.py:130
  35.4 0.9 %collective-permute-done.12.got = bf16[2,2,160,128]{3,2,1,0:T(8,128)(2,1)S(1)} collective-permute-done((bf16[2,2,160,128]{3,2,1,0:T(8,128)(2,1)S(1)}, bf16[2,2,160,128]{3,2,1,0:T(8,128)(2,1)S(1)}, u32[]{:S(2)}, u32[]{:S(2)}) %collective-permute-start.12) | collective-permute-done | bytes 163872 | tf_op jit(solution)/shard_map/ppermute | solution.py:44
  36.3 3.1 %collective-permute-start.13 = (bf16[2,2,160,128]{3,2,1,0:T(8,128)(2,1)S(1)}, bf16[2,2,160,128]{3,2,1,0:T(8,128)(2,1)S(1)}, u32[]{:S(2)}, u32[]{:S(2)}) collective-permute-start(bf16[2,2,160,128]{3,2,1,0:T(8,128)(2,1)S(1)} %get-tuple-element.56), channel_id=1, source_target_pairs={{0,28},{1,25},{2,30},{3,27},{4,24},{5,29},{6,26},{7,31},{8,20},{9,... | collective-permute-start | bytes 491528 | tf_op jit(solution)/shard_map/ppermute | solution.py:57
  40.1 1.8 %collective-permute-start.18 = (bf16[2,2,160,128]{3,2,1,0:T(8,128)(2,1)S(1)}, bf16[2,2,160,128]{3,2,1,0:T(8,128)(2,1)S(1)}, u32[]{:S(2)}, u32[]{:S(2)}) collective-permute-start(bf16[2,2,160,128]{3,2,1,0:T(8,128)(2,1)S(1)} %get-tuple-element.61), channel_id=1, source_target_pairs={{0,4},{1,13},{2,6},{3,15},{4,0},{5,9},{6,2},{7,11},{8,12},{9,5},{1... | collective-permute-start | bytes 491528 | tf_op jit(solution)/shard_map/ppermute | solution.py:57
  41.9 1.4 %collective-permute-start.20 = (bf16[2,2,160,128]{3,2,1,0:T(8,128)(2,1)S(1)}, bf16[2,2,160,128]{3,2,1,0:T(8,128)(2,1)S(1)}, u32[]{:S(2)}, u32[]{:S(2)}) collective-permute-start(bf16[2,2,160,128]{3,2,1,0:T(8,128)(2,1)S(1)} %get-tuple-element.62.own), channel_id=1, source_target_pairs={{0,2},{2,0},{1,3},{3,1},{4,6},{6,4},{5,7},{7,5},{8,10},{10,8},{9,1... | collective-permute-start | bytes 491528 | tf_op jit(solution)/shard_map/ppermute | solution.py:44
  43.3 2.8 %collective-permute-done.13.own = bf16[2,2,160,128]{3,2,1,0:T(8,128)(2,1)S(1)} collective-permute-done((bf16[2,2,160,128]{3,2,1,0:T(8,128)(2,1)S(1)}, bf16[2,2,160,128]{3,2,1,0:T(8,128)(2,1)S(1)}, u32[]{:S(2)}, u32[]{:S(2)}) %collective-permute-start.13) | collective-permute-done | bytes 163872 | tf_op jit(solution)/shard_map/ppermute | solution.py:57
  46.2 1.4 %collective-permute-start.14 = (bf16[2,2,160,128]{3,2,1,0:T(8,128)(2,1)S(1)}, bf16[2,2,160,128]{3,2,1,0:T(8,128)(2,1)S(1)}, u32[]{:S(2)}, u32[]{:S(2)}) collective-permute-start(bf16[2,2,160,128]{3,2,1,0:T(8,128)(2,1)S(1)} %collective-permute-done.13.own), channel_id=1, source_target_pairs={{0,2},{2,0},{1,3},{3,1},{4,6},{6,4},{5,7},{7,5},{8,10},{10,8},{9,1... | collective-permute-start | bytes 491528 | tf_op jit(solution)/shard_map/ppermute | solution.py:44
  47.6 2.3 %collective-permute-start.17 = (bf16[2,2,160,128]{3,2,1,0:T(8,128)(2,1)S(1)}, bf16[2,2,160,128]{3,2,1,0:T(8,128)(2,1)S(1)}, u32[]{:S(2)}, u32[]{:S(2)}) collective-permute-start(bf16[2,2,160,128]{3,2,1,0:T(8,128)(2,1)S(1)} %fold.12), channel_id=1, source_target_pairs={{0,16},{1,21},{2,18},{3,23},{4,20},{5,17},{6,22},{7,19},{8,24},{9,... | collective-permute-start | bytes 491528 | tf_op jit(solution)/shard_map/ppermute | solution.py:57
  50.0 0.8 %collective-permute-start.19 = (bf16[2,2,160,128]{3,2,1,0:T(8,128)(2,1)S(1)}, bf16[2,2,160,128]{3,2,1,0:T(8,128)(2,1)S(1)}, u32[]{:S(2)}, u32[]{:S(2)}) collective-permute-start(bf16[2,2,160,128]{3,2,1,0:T(8,128)(2,1)S(1)} %collective-permute-done.18.own), channel_id=1, source_target_pairs={{0,2},{2,0},{1,3},{3,1},{4,6},{6,4},{5,7},{7,5},{8,10},{10,8},{9,1... | collective-permute-start | bytes 491528 | tf_op jit(solution)/shard_map/ppermute | solution.py:44
  51.5 2.1 %collective-permute-done.14.peer = bf16[2,2,160,128]{3,2,1,0:T(8,128)(2,1)S(1)} collective-permute-done((bf16[2,2,160,128]{3,2,1,0:T(8,128)(2,1)S(1)}, bf16[2,2,160,128]{3,2,1,0:T(8,128)(2,1)S(1)}, u32[]{:S(2)}, u32[]{:S(2)}) %collective-permute-start.14) | collective-permute-done | bytes 163872 | tf_op jit(solution)/shard_map/ppermute | solution.py:44
  53.6 2.7 %collective-permute-done.17.refs_2_ = bf16[2,2,160,128]{3,2,1,0:T(8,128)(2,1)S(1)} collective-permute-done((bf16[2,2,160,128]{3,2,1,0:T(8,128)(2,1)S(1)}, bf16[2,2,160,128]{3,2,1,0:T(8,128)(2,1)S(1)}, u32[]{:S(2)}, u32[]{:S(2)}) %collective-permute-start.17) | collective-permute-done | bytes 163872 | tf_op jit(solution)/shard_map/ppermute | solution.py:57
  56.7 1.6 %collective-permute-done.23.got = bf16[4,2,160,128]{3,2,1,0:T(8,128)(2,1)S(1)} collective-permute-done((bf16[4,2,160,128]{3,2,1,0:T(8,128)(2,1)S(1)}, bf16[4,2,160,128]{3,2,1,0:T(8,128)(2,1)S(1)}, u32[]{:S(2)}, u32[]{:S(2)}) %collective-permute-start.23) | collective-permute-done | bytes 327712 | tf_op jit(solution)/shard_map/ppermute | solution.py:44
  58.3 1.8 %place.1 = (bf16[160,16,128]{2,1,0:T(8,128)(2,1)}, bf16[640,512]{1,0:T(8,128)(2,1)}) custom-call(s32[16]{0:T(128)S(1)} %copy-done.4, bf16[4,2,160,128]{3,2,1,0:T(8,128)(2,1)S(1)} %get-tuple-element.66.keep, bf16[4,2,160,128]{3,2,1,0:T(8,128)(2,1)S(1)} %collective-permute-done.23.got, bf16[640,256]{1,0:T(8,128)(2,1)S(1)} %get-tuple-element.68.spec_mine, ...), custom_call_target="tpu_custom_call" | custom-call | bytes 2621504 | tf_op jit(solution)/shard_map/place/pallas_call | solution.py:130
  (56 shorter events, 9.0 us)
Async XLA Ops:
  4.6 1.5 %collective-permute-start = (bf16[2,2,160,128]{3,2,1,0:T(8,128)(2,1)S(1)}, bf16[2,2,160,128]{3,2,1,0:T(8,128)(2,1)S(1)}, u32[]{:S(2)}, u32[]{:S(2)}) collective-permute-start(bf16[2,2,160,128]{3,2,1,0:T(8,128)(2,1)S(1)} %get-tuple-element.38), channel_id=1, source_target_pairs={{0,1},{1,0},{2,3},{3,2},{4,5},{5,4},{6,7},{7,6},{8,9},{9,8},{10,11... | collective-permute-start | bytes 491528 | tf_op jit(solution)/shard_map/ppermute | solution.py:44
  5.1 1.4 %collective-permute-start.3 = (bf16[2,2,160,128]{3,2,1,0:T(8,128)(2,1)S(1)}, bf16[2,2,160,128]{3,2,1,0:T(8,128)(2,1)S(1)}, u32[]{:S(2)}, u32[]{:S(2)}) collective-permute-start(bf16[2,2,160,128]{3,2,1,0:T(8,128)(2,1)S(1)} %get-tuple-element.41), channel_id=1, source_target_pairs={{0,1},{1,0},{2,3},{3,2},{4,5},{5,4},{6,7},{7,6},{8,9},{9,8},{10,11... | collective-permute-start | bytes 491528 | tf_op jit(solution)/shard_map/ppermute | solution.py:44
  6.5 22.3 %collective-permute-start.10 = (bf16[2,1,640,1280]{3,2,1,0:T(8,128)(2,1)}, bf16[2,1,640,1280]{3,2,1,0:T(8,128)(2,1)S(1)}, u32[]{:S(2)}, u32[]{:S(2)}) collective-permute-start(bf16[2,1,640,1280]{3,2,1,0:T(8,128)(2,1)} %tables_mine.1), channel_id=1, source_target_pairs={{0,1},{1,0},{2,3},{3,2},{4,5},{5,4},{6,7},{7,6},{8,9},{9,8},{10,11... | collective-permute-start | bytes 9830408 | tf_op jit(solution)/shard_map/ppermute | solution.py:44
  6.8 10.9 %collective-permute-start.1 = (bf16[2,2,160,128]{3,2,1,0:T(8,128)(2,1)S(1)}, bf16[2,2,160,128]{3,2,1,0:T(8,128)(2,1)S(1)}, u32[]{:S(2)}, u32[]{:S(2)}) collective-permute-start(bf16[2,2,160,128]{3,2,1,0:T(8,128)(2,1)S(1)} %get-tuple-element.39), channel_id=1, source_target_pairs={{0,28},{1,25},{2,30},{3,27},{4,24},{5,29},{6,26},{7,31},{8,20},{9,... | collective-permute-start | bytes 491528 | tf_op jit(solution)/shard_map/ppermute | solution.py:57
  12.7 7.2 %collective-permute-start.4 = (bf16[2,2,160,128]{3,2,1,0:T(8,128)(2,1)S(1)}, bf16[2,2,160,128]{3,2,1,0:T(8,128)(2,1)S(1)}, u32[]{:S(2)}, u32[]{:S(2)}) collective-permute-start(bf16[2,2,160,128]{3,2,1,0:T(8,128)(2,1)S(1)} %get-tuple-element.42.own), channel_id=1, source_target_pairs={{0,2},{2,0},{1,3},{3,1},{4,6},{6,4},{5,7},{7,5},{8,10},{10,8},{9,1... | collective-permute-start | bytes 491528 | tf_op jit(solution)/shard_map/ppermute | solution.py:44
  14.2 8.9 %collective-permute-start.6 = (bf16[2,2,160,128]{3,2,1,0:T(8,128)(2,1)S(1)}, bf16[2,2,160,128]{3,2,1,0:T(8,128)(2,1)S(1)}, u32[]{:S(2)}, u32[]{:S(2)}) collective-permute-start(bf16[2,2,160,128]{3,2,1,0:T(8,128)(2,1)S(1)} %get-tuple-element.44), channel_id=1, source_target_pairs={{0,4},{1,13},{2,6},{3,15},{4,0},{5,9},{6,2},{7,11},{8,12},{9,5},{1... | collective-permute-start | bytes 491528 | tf_op jit(solution)/shard_map/ppermute | solution.py:57
  14.8 8.9 %collective-permute-start.8 = (bf16[2,2,160,128]{3,2,1,0:T(8,128)(2,1)S(1)}, bf16[2,2,160,128]{3,2,1,0:T(8,128)(2,1)S(1)}, u32[]{:S(2)}, u32[]{:S(2)}) collective-permute-start(bf16[2,2,160,128]{3,2,1,0:T(8,128)(2,1)S(1)} %get-tuple-element.45.own), channel_id=1, source_target_pairs={{0,2},{2,0},{1,3},{3,1},{4,6},{6,4},{5,7},{7,5},{8,10},{10,8},{9,1... | collective-permute-start | bytes 491528 | tf_op jit(solution)/shard_map/ppermute | solution.py:44
  17.7 7.5 %collective-permute-start.2 = (bf16[2,2,160,128]{3,2,1,0:T(8,128)(2,1)S(1)}, bf16[2,2,160,128]{3,2,1,0:T(8,128)(2,1)S(1)}, u32[]{:S(2)}, u32[]{:S(2)}) collective-permute-start(bf16[2,2,160,128]{3,2,1,0:T(8,128)(2,1)S(1)} %collective-permute-done.1.own), channel_id=1, source_target_pairs={{0,2},{2,0},{1,3},{3,1},{4,6},{6,4},{5,7},{7,5},{8,10},{10,8},{9,1... | collective-permute-start | bytes 491528 | tf_op jit(solution)/shard_map/ppermute | solution.py:44
  19.9 8.8 %collective-permute-start.5 = (bf16[2,2,160,128]{3,2,1,0:T(8,128)(2,1)S(1)}, bf16[2,2,160,128]{3,2,1,0:T(8,128)(2,1)S(1)}, u32[]{:S(2)}, u32[]{:S(2)}) collective-permute-start(bf16[2,2,160,128]{3,2,1,0:T(8,128)(2,1)S(1)} %fold.8), channel_id=1, source_target_pairs={{0,16},{1,21},{2,18},{3,23},{4,20},{5,17},{6,22},{7,19},{8,24},{9,... | collective-permute-start | bytes 491528 | tf_op jit(solution)/shard_map/ppermute | solution.py:57
  23.1 5.6 %collective-permute-start.7 = (bf16[2,2,160,128]{3,2,1,0:T(8,128)(2,1)S(1)}, bf16[2,2,160,128]{3,2,1,0:T(8,128)(2,1)S(1)}, u32[]{:S(2)}, u32[]{:S(2)}) collective-permute-start(bf16[2,2,160,128]{3,2,1,0:T(8,128)(2,1)S(1)} %collective-permute-done.6.own), channel_id=1, source_target_pairs={{0,2},{2,0},{1,3},{3,1},{4,6},{6,4},{5,7},{7,5},{8,10},{10,8},{9,1... | collective-permute-start | bytes 491528 | tf_op jit(solution)/shard_map/ppermute | solution.py:44
  23.8 5.1 %collective-permute-start.9 = (bf16[2,2,160,128]{3,2,1,0:T(8,128)(2,1)S(1)}, bf16[2,2,160,128]{3,2,1,0:T(8,128)(2,1)S(1)}, u32[]{:S(2)}, u32[]{:S(2)}) collective-permute-start(bf16[2,2,160,128]{3,2,1,0:T(8,128)(2,1)S(1)} %fold.11.refs_4_), channel_id=1, source_target_pairs={{1,9},{3,11},{5,13},{7,15},{9,1},{11,3},{13,5},{15,7},{17,25},{19,... | collective-permute-start | bytes 491528 | tf_op jit(solution)/shard_map/ppermute | solution.py:57
  29.0 1.8 %collective-permute-start.11 = (bf16[4,2,160,128]{3,2,1,0:T(8,128)(2,1)S(1)}, bf16[4,2,160,128]{3,2,1,0:T(8,128)(2,1)S(1)}, u32[]{:S(2)}, u32[]{:S(2)}) collective-permute-start(bf16[4,2,160,128]{3,2,1,0:T(8,128)(2,1)S(1)} %get-tuple-element.49), channel_id=1, source_target_pairs={{0,1},{1,0},{2,3},{3,2},{4,5},{5,4},{6,7},{7,6},{8,9},{9,8},{10,11... | collective-permute-start | bytes 983048 | tf_op jit(solution)/shard_map/ppermute | solution.py:44
  34.8 1.5 %collective-permute-start.12 = (bf16[2,2,160,128]{3,2,1,0:T(8,128)(2,1)S(1)}, bf16[2,2,160,128]{3,2,1,0:T(8,128)(2,1)S(1)}, u32[]{:S(2)}, u32[]{:S(2)}) collective-permute-start(bf16[2,2,160,128]{3,2,1,0:T(8,128)(2,1)S(1)} %get-tuple-element.55), channel_id=1, source_target_pairs={{0,1},{1,0},{2,3},{3,2},{4,5},{5,4},{6,7},{7,6},{8,9},{9,8},{10,11... | collective-permute-start | bytes 491528 | tf_op jit(solution)/shard_map/ppermute | solution.py:44
  35.3 4.2 %collective-permute-start.15 = (bf16[2,2,160,128]{3,2,1,0:T(8,128)(2,1)S(1)}, bf16[2,2,160,128]{3,2,1,0:T(8,128)(2,1)S(1)}, u32[]{:S(2)}, u32[]{:S(2)}) collective-permute-start(bf16[2,2,160,128]{3,2,1,0:T(8,128)(2,1)S(1)} %get-tuple-element.58), channel_id=1, source_target_pairs={{0,1},{1,0},{2,3},{3,2},{4,5},{5,4},{6,7},{7,6},{8,9},{9,8},{10,11... | collective-permute-start | bytes 491528 | tf_op jit(solution)/shard_map/ppermute | solution.py:44
  36.3 9.8 %collective-permute-start.13 = (bf16[2,2,160,128]{3,2,1,0:T(8,128)(2,1)S(1)}, bf16[2,2,160,128]{3,2,1,0:T(8,128)(2,1)S(1)}, u32[]{:S(2)}, u32[]{:S(2)}) collective-permute-start(bf16[2,2,160,128]{3,2,1,0:T(8,128)(2,1)S(1)} %get-tuple-element.56), channel_id=1, source_target_pairs={{0,28},{1,25},{2,30},{3,27},{4,24},{5,29},{6,26},{7,31},{8,20},{9,... | collective-permute-start | bytes 491528 | tf_op jit(solution)/shard_map/ppermute | solution.py:57
  39.5 8.1 %collective-permute-start.16 = (bf16[2,2,160,128]{3,2,1,0:T(8,128)(2,1)S(1)}, bf16[2,2,160,128]{3,2,1,0:T(8,128)(2,1)S(1)}, u32[]{:S(2)}, u32[]{:S(2)}) collective-permute-start(bf16[2,2,160,128]{3,2,1,0:T(8,128)(2,1)S(1)} %get-tuple-element.59.own), channel_id=1, source_target_pairs={{0,2},{2,0},{1,3},{3,1},{4,6},{6,4},{5,7},{7,5},{8,10},{10,8},{9,1... | collective-permute-start | bytes 491528 | tf_op jit(solution)/shard_map/ppermute | solution.py:44
  40.1 16.2 %collective-permute-start.22 = (bf16[640,256]{1,0:T(8,128)(2,1)S(1)}, bf16[640,256]{1,0:T(8,128)(2,1)S(1)}, u32[]{:S(2)}, u32[]{:S(2)}) collective-permute-start(bf16[640,256]{1,0:T(8,128)(2,1)S(1)} %get-tuple-element.64), channel_id=1, source_target_pairs={{0,1},{1,0},{2,3},{3,2},{4,5},{5,4},{6,7},{7,6},{8,9},{9,8},{10,11... | collective-permute-start | bytes 983048 | tf_op jit(solution)/shard_map/ppermute | solution.py:44
  40.1 9.8 %collective-permute-start.18 = (bf16[2,2,160,128]{3,2,1,0:T(8,128)(2,1)S(1)}, bf16[2,2,160,128]{3,2,1,0:T(8,128)(2,1)S(1)}, u32[]{:S(2)}, u32[]{:S(2)}) collective-permute-start(bf16[2,2,160,128]{3,2,1,0:T(8,128)(2,1)S(1)} %get-tuple-element.61), channel_id=1, source_target_pairs={{0,4},{1,13},{2,6},{3,15},{4,0},{5,9},{6,2},{7,11},{8,12},{9,5},{1... | collective-permute-start | bytes 491528 | tf_op jit(solution)/shard_map/ppermute | solution.py:57
  41.9 8.8 %collective-permute-start.20 = (bf16[2,2,160,128]{3,2,1,0:T(8,128)(2,1)S(1)}, bf16[2,2,160,128]{3,2,1,0:T(8,128)(2,1)S(1)}, u32[]{:S(2)}, u32[]{:S(2)}) collective-permute-start(bf16[2,2,160,128]{3,2,1,0:T(8,128)(2,1)S(1)} %get-tuple-element.62.own), channel_id=1, source_target_pairs={{0,2},{2,0},{1,3},{3,1},{4,6},{6,4},{5,7},{7,5},{8,10},{10,8},{9,1... | collective-permute-start | bytes 491528 | tf_op jit(solution)/shard_map/ppermute | solution.py:44
  46.2 7.5 %collective-permute-start.14 = (bf16[2,2,160,128]{3,2,1,0:T(8,128)(2,1)S(1)}, bf16[2,2,160,128]{3,2,1,0:T(8,128)(2,1)S(1)}, u32[]{:S(2)}, u32[]{:S(2)}) collective-permute-start(bf16[2,2,160,128]{3,2,1,0:T(8,128)(2,1)S(1)} %collective-permute-done.13.own), channel_id=1, source_target_pairs={{0,2},{2,0},{1,3},{3,1},{4,6},{6,4},{5,7},{7,5},{8,10},{10,8},{9,1... | collective-permute-start | bytes 491528 | tf_op jit(solution)/shard_map/ppermute | solution.py:44
  47.6 8.7 %collective-permute-start.17 = (bf16[2,2,160,128]{3,2,1,0:T(8,128)(2,1)S(1)}, bf16[2,2,160,128]{3,2,1,0:T(8,128)(2,1)S(1)}, u32[]{:S(2)}, u32[]{:S(2)}) collective-permute-start(bf16[2,2,160,128]{3,2,1,0:T(8,128)(2,1)S(1)} %fold.12), channel_id=1, source_target_pairs={{0,16},{1,21},{2,18},{3,23},{4,20},{5,17},{6,22},{7,19},{8,24},{9,... | collective-permute-start | bytes 491528 | tf_op jit(solution)/shard_map/ppermute | solution.py:57
  50.0 6.4 %collective-permute-start.19 = (bf16[2,2,160,128]{3,2,1,0:T(8,128)(2,1)S(1)}, bf16[2,2,160,128]{3,2,1,0:T(8,128)(2,1)S(1)}, u32[]{:S(2)}, u32[]{:S(2)}) collective-permute-start(bf16[2,2,160,128]{3,2,1,0:T(8,128)(2,1)S(1)} %collective-permute-done.18.own), channel_id=1, source_target_pairs={{0,2},{2,0},{1,3},{3,1},{4,6},{6,4},{5,7},{7,5},{8,10},{10,8},{9,1... | collective-permute-start | bytes 491528 | tf_op jit(solution)/shard_map/ppermute | solution.py:44
  50.8 5.7 %collective-permute-start.21 = (bf16[2,2,160,128]{3,2,1,0:T(8,128)(2,1)S(1)}, bf16[2,2,160,128]{3,2,1,0:T(8,128)(2,1)S(1)}, u32[]{:S(2)}, u32[]{:S(2)}) collective-permute-start(bf16[2,2,160,128]{3,2,1,0:T(8,128)(2,1)S(1)} %fold.15.refs_4_), channel_id=1, source_target_pairs={{1,9},{3,11},{5,13},{7,15},{9,1},{11,3},{13,5},{15,7},{17,25},{19,... | collective-permute-start | bytes 491528 | tf_op jit(solution)/shard_map/ppermute | solution.py:57
  56.6 1.7 %collective-permute-start.23 = (bf16[4,2,160,128]{3,2,1,0:T(8,128)(2,1)S(1)}, bf16[4,2,160,128]{3,2,1,0:T(8,128)(2,1)S(1)}, u32[]{:S(2)}, u32[]{:S(2)}) collective-permute-start(bf16[4,2,160,128]{3,2,1,0:T(8,128)(2,1)S(1)} %get-tuple-element.67), channel_id=1, source_target_pairs={{0,1},{1,0},{2,3},{3,2},{4,5},{5,4},{6,7},{7,6},{8,9},{9,8},{10,11... | collective-permute-start | bytes 983048 | tf_op jit(solution)/shard_map/ppermute | solution.py:44
  (7 other events, 111.4 us)

commit v4 on v3

--- a/solution.py
+++ b/solution.py
@@ -230,29 +230,13 @@
     column = lax.broadcasted_iota(jnp.int32, (width, width), 1)
     same = ((row + column) & 1) == 0
 
-    def widen(square):
-        tall = jnp.dot(spread_16, square, preferred_element_type=f32).astype(bf16)
+    for square, out in ((to_modes, to_wide), (from_modes, from_wide)):
+        tall = jnp.dot(spread_16, square[...].astype(bf16), preferred_element_type=f32)
         wide = lax.dot_general(
-            tall, spread_16, (((1,), (1,)), ((), ())), preferred_element_type=f32
+            tall.astype(bf16), spread_16, (((1,), (1,)), ((), ())), preferred_element_type=f32
         )
-        return jnp.where(same, wide, 0.0).astype(bf16)
-
-    for square, out in ((to_modes, to_wide), (from_modes, from_wide)):
-        high = square[...].astype(bf16)
-        low = (square[...] - high.astype(f32)).astype(bf16)
-        wide = widen(high)
-        out[:, 0:width] = wide
-        out[:, width : 2 * width] = wide
-        out[:, 2 * width :] = widen(low)
+        out[...] = jnp.where(same, wide, 0.0).astype(bf16)
     rate[...] = jnp.sum(spread * rates[...], axis=1, keepdims=True)
-
-
-def product_3(wide, value):
-    high = value.astype(jnp.bfloat16)
-    low = (value - high.astype(jnp.float32)).astype(jnp.bfloat16)
-    return jnp.dot(
-        wide[...], jnp.concatenate([high, low, high], axis=0), preferred_element_type=jnp.float32
-    )
 
 
 def solve_kernel(
@@ -286,8 +270,11 @@
     kept = jnp.where(degree <= top_degree, raw, 0.0)
     degree_f = degree.astype(jnp.float32)
     stiffness = degree_f * (degree_f + 1.0) / (top_degree * (top_degree + 1.0))
-    damped = product_3(to_wide, kept) / (1.0 + stiffness * rate[...])
-    updated = product_3(from_wide, damped)
+    modal = jnp.dot(to_wide[...], kept.astype(jnp.bfloat16), preferred_element_type=jnp.float32)
+    damped = modal / (1.0 + stiffness * rate[...])
+    updated = jnp.dot(
+        from_wide[...], damped.astype(jnp.bfloat16), preferred_element_type=jnp.float32
+    )
     spec[...] = jnp.transpose(updated.astype(jnp.bfloat16))
     for at, table in ((at_mine, table_mine), (at_other, table_other)):
         parts[at, :] = jnp.dot(
@@ -376,7 +363,7 @@
         *scaled, lambda tie: swap(lax.optimization_barrier((legendre, *tie))[0], "lev"), plan
     )
 
-    wide = jax.ShapeDtypeStruct((width, 3 * width), bf16)
+    wide = jax.ShapeDtypeStruct((width, width), bf16)
     to_wide, from_wide, rate = call(
         widen_kernel, (wide, wide, jax.ShapeDtypeStruct((width, 1), f32)), "widen", 8
     )(to_modes, from_modes, mode_rates[None, :])

time: 60.2 us -> 59.7 us (level)
  Pallas kernels: 8.48 us -> 7.78 us
    pallas_call x18, Pallas kernels: 8.48 us -> 7.78 us  [run(): pl.pallas_call(kernel, out_shape=shapes, in_specs=in_specs or [VMEM] * le...]
where the time goes in v4:
time: 59.7 us; the launch traced here: 59.5 us
  starting transfers between devices  28.9 us (48%)
  waiting for transfers between devices  19.5 us (33%)
  Pallas kernels  7.78 us (13%)
  local copies, waits for them, and re-layouts  2.58 us (4%)
  between operations  0.82 us (1%)
    ppermute x8, starting transfers between devices, meet(): return lax.ppermute(value, AXES, pairs)  18.2 us
    ppermute x8, waiting for transfers between devices, meet(): return lax.ppermute(value, AXES, pairs)  11.5 us
    ppermute x16, starting transfers between devices, swap(): return lax.ppermute(value, axis, [(0, 1), (1, 0)])  10.7 us
    ppermute x16, waiting for transfers between devices, swap(): return lax.ppermute(value, axis, [(0, 1), (1, 0)])  7.97 us
    pallas_call x18, Pallas kernels, run(): pl.pallas_call(kernel, out_shape=shapes, in_specs=in_specs or [VMEM] * le...  7.78 us
    unnamed x14, local copies, waits for them, and re-layouts  2.58 us
  transfers between devices with their start and end apart: 24, of which 12 were waited for; matrix products, arithmetic and copies ran while one was open for 0% of the time, Pallas kernels for 2%

profile of v4, /device:TPU:0, one launch (start us, length us, event | category | flops | bytes accessed | tf_op | source)
XLA Modules:
  0.0 59.5 jit_solution(2769018708252620525)
XLA Ops:
  0.7 1.2 %copy-done.1 = bf16[1,160,16,128]{3,2,1,0:T(8,128)(2,1)S(1)} copy-done((bf16[1,160,16,128]{3,2,1,0:T(8,128)(2,1)S(1)}, bf16[1,160,16,128]{3,2,1,0:T(8,128)(2,1)}, u32[]{:S(2)}) %copy-start.1) | copy-done | bytes 655384
  3.2 1.4 %scale.1 = (bf16[2,2,160,128]{3,2,1,0:T(8,128)(2,1)S(1)}, bf16[2,2,160,128]{3,2,1,0:T(8,128)(2,1)S(1)}, bf16[2,2,160,128]{3,2,1,0:T(8,128)(2,1)S(1)}, bf16[2,2,160,128]{3,2,1,0:T(8,128)(2,1)S(1)}) custom-call(s32[16]{0:T(128)S(1)} %copy-done.4, bf16[160,16,128]{2,1,0:T(8,128)(2,1)S(1)} %bitcast.5, f32[1,160]{1,0:T(1,128)S(1)} %bitcast.6), custom_call_target="tpu_custom_call" | custom-call | bytes 1311424 | tf_op jit(solution)/shard_map/scale/pallas_call | solution.py:130
  5.2 0.9 %collective-permute-done.got = bf16[2,2,160,128]{3,2,1,0:T(8,128)(2,1)S(1)} collective-permute-done((bf16[2,2,160,128]{3,2,1,0:T(8,128)(2,1)S(1)}, bf16[2,2,160,128]{3,2,1,0:T(8,128)(2,1)S(1)}, u32[]{:S(2)}, u32[]{:S(2)}) %collective-permute-start) | collective-permute-done | bytes 163872 | tf_op jit(solution)/shard_map/ppermute | solution.py:44
  6.8 5.9 %collective-permute-start.1 = (bf16[2,2,160,128]{3,2,1,0:T(8,128)(2,1)S(1)}, bf16[2,2,160,128]{3,2,1,0:T(8,128)(2,1)S(1)}, u32[]{:S(2)}, u32[]{:S(2)}) collective-permute-start(bf16[2,2,160,128]{3,2,1,0:T(8,128)(2,1)S(1)} %get-tuple-element.39), channel_id=1, source_target_pairs={{0,28},{1,25},{2,30},{3,27},{4,24},{5,29},{6,26},{7,31},{8,20},{9,... | collective-permute-start | bytes 491528 | tf_op jit(solution)/shard_map/ppermute | solution.py:57
  12.7 1.6 %collective-permute-start.4 = (bf16[2,2,160,128]{3,2,1,0:T(8,128)(2,1)S(1)}, bf16[2,2,160,128]{3,2,1,0:T(8,128)(2,1)S(1)}, u32[]{:S(2)}, u32[]{:S(2)}) collective-permute-start(bf16[2,2,160,128]{3,2,1,0:T(8,128)(2,1)S(1)} %get-tuple-element.42.own), channel_id=1, source_target_pairs={{0,2},{2,0},{1,3},{3,1},{4,6},{6,4},{5,7},{7,5},{8,10},{10,8},{9,1... | collective-permute-start | bytes 491528 | tf_op jit(solution)/shard_map/ppermute | solution.py:44
  15.3 2.4 %collective-permute-done.1.own = bf16[2,2,160,128]{3,2,1,0:T(8,128)(2,1)S(1)} collective-permute-done((bf16[2,2,160,128]{3,2,1,0:T(8,128)(2,1)S(1)}, bf16[2,2,160,128]{3,2,1,0:T(8,128)(2,1)S(1)}, u32[]{:S(2)}, u32[]{:S(2)}) %collective-permute-start.1) | collective-permute-done | bytes 163872 | tf_op jit(solution)/shard_map/ppermute | solution.py:57
  17.7 1.8 %collective-permute-start.2 = (bf16[2,2,160,128]{3,2,1,0:T(8,128)(2,1)S(1)}, bf16[2,2,160,128]{3,2,1,0:T(8,128)(2,1)S(1)}, u32[]{:S(2)}, u32[]{:S(2)}) collective-permute-start(bf16[2,2,160,128]{3,2,1,0:T(8,128)(2,1)S(1)} %collective-permute-done.1.own), channel_id=1, source_target_pairs={{0,2},{2,0},{1,3},{3,1},{4,6},{6,4},{5,7},{7,5},{8,10},{10,8},{9,1... | collective-permute-start | bytes 491528 | tf_op jit(solution)/shard_map/ppermute | solution.py:44
  19.9 3.2 %collective-permute-start.5 = (bf16[2,2,160,128]{3,2,1,0:T(8,128)(2,1)S(1)}, bf16[2,2,160,128]{3,2,1,0:T(8,128)(2,1)S(1)}, u32[]{:S(2)}, u32[]{:S(2)}) collective-permute-start(bf16[2,2,160,128]{3,2,1,0:T(8,128)(2,1)S(1)} %fold.8), channel_id=1, source_target_pairs={{0,16},{1,21},{2,18},{3,23},{4,20},{5,17},{6,22},{7,19},{8,24},{9,... | collective-permute-start | bytes 491528 | tf_op jit(solution)/shard_map/ppermute | solution.py:57
  24.4 0.7 %collective-permute-done.2.peer = bf16[2,2,160,128]{3,2,1,0:T(8,128)(2,1)S(1)} collective-permute-done((bf16[2,2,160,128]{3,2,1,0:T(8,128)(2,1)S(1)}, bf16[2,2,160,128]{3,2,1,0:T(8,128)(2,1)S(1)}, u32[]{:S(2)}, u32[]{:S(2)}) %collective-permute-start.2) | collective-permute-done | bytes 163872 | tf_op jit(solution)/shard_map/ppermute | solution.py:44
  25.1 3.6 %collective-permute-done.5.refs_2_ = bf16[2,2,160,128]{3,2,1,0:T(8,128)(2,1)S(1)} collective-permute-done((bf16[2,2,160,128]{3,2,1,0:T(8,128)(2,1)S(1)}, bf16[2,2,160,128]{3,2,1,0:T(8,128)(2,1)S(1)}, u32[]{:S(2)}, u32[]{:S(2)}) %collective-permute-start.5) | collective-permute-done | bytes 163872 | tf_op jit(solution)/shard_map/ppermute | solution.py:57
  29.8 0.9 %collective-permute-done.11.got = bf16[4,2,160,128]{3,2,1,0:T(8,128)(2,1)S(1)} collective-permute-done((bf16[4,2,160,128]{3,2,1,0:T(8,128)(2,1)S(1)}, bf16[4,2,160,128]{3,2,1,0:T(8,128)(2,1)S(1)}, u32[]{:S(2)}, u32[]{:S(2)}) %collective-permute-start.11) | collective-permute-done | bytes 327712 | tf_op jit(solution)/shard_map/ppermute | solution.py:44
  30.7 3.6 %solve.1 = (bf16[640,256]{1,0:T(8,128)(2,1)S(1)}, bf16[640,256]{1,0:T(8,128)(2,1)S(1)}, bf16[2,2,160,128]{3,2,1,0:T(8,128)(2,1)S(1)}, bf16[2,2,160,128]{3,2,1,0:...) custom-call(s32[16]{0:T(128)S(1)} %copy-done.4, ...), custom_call_target="tpu_custom_call" | custom-call | bytes 8782912 | tf_op jit(solution)/shard_map/solve/pallas_call | solution.py:130
  34.9 0.9 %collective-permute-done.12.got = bf16[2,2,160,128]{3,2,1,0:T(8,128)(2,1)S(1)} collective-permute-done((bf16[2,2,160,128]{3,2,1,0:T(8,128)(2,1)S(1)}, bf16[2,2,160,128]{3,2,1,0:T(8,128)(2,1)S(1)}, u32[]{:S(2)}, u32[]{:S(2)}) %collective-permute-start.12) | collective-permute-done | bytes 163872 | tf_op jit(solution)/shard_map/ppermute | solution.py:44
  35.8 3.1 %collective-permute-start.13 = (bf16[2,2,160,128]{3,2,1,0:T(8,128)(2,1)S(1)}, bf16[2,2,160,128]{3,2,1,0:T(8,128)(2,1)S(1)}, u32[]{:S(2)}, u32[]{:S(2)}) collective-permute-start(bf16[2,2,160,128]{3,2,1,0:T(8,128)(2,1)S(1)} %get-tuple-element.56), channel_id=1, source_target_pairs={{0,28},{1,25},{2,30},{3,27},{4,24},{5,29},{6,26},{7,31},{8,20},{9,... | collective-permute-start | bytes 491528 | tf_op jit(solution)/shard_map/ppermute | solution.py:57
  39.6 1.8 %collective-permute-start.18 = (bf16[2,2,160,128]{3,2,1,0:T(8,128)(2,1)S(1)}, bf16[2,2,160,128]{3,2,1,0:T(8,128)(2,1)S(1)}, u32[]{:S(2)}, u32[]{:S(2)}) collective-permute-start(bf16[2,2,160,128]{3,2,1,0:T(8,128)(2,1)S(1)} %get-tuple-element.61), channel_id=1, source_target_pairs={{0,4},{1,13},{2,6},{3,15},{4,0},{5,9},{6,2},{7,11},{8,12},{9,5},{1... | collective-permute-start | bytes 491528 | tf_op jit(solution)/shard_map/ppermute | solution.py:57
  41.4 1.4 %collective-permute-start.20 = (bf16[2,2,160,128]{3,2,1,0:T(8,128)(2,1)S(1)}, bf16[2,2,160,128]{3,2,1,0:T(8,128)(2,1)S(1)}, u32[]{:S(2)}, u32[]{:S(2)}) collective-permute-start(bf16[2,2,160,128]{3,2,1,0:T(8,128)(2,1)S(1)} %get-tuple-element.62.own), channel_id=1, source_target_pairs={{0,2},{2,0},{1,3},{3,1},{4,6},{6,4},{5,7},{7,5},{8,10},{10,8},{9,1... | collective-permute-start | bytes 491528 | tf_op jit(solution)/shard_map/ppermute | solution.py:44
  42.8 2.8 %collective-permute-done.13.own = bf16[2,2,160,128]{3,2,1,0:T(8,128)(2,1)S(1)} collective-permute-done((bf16[2,2,160,128]{3,2,1,0:T(8,128)(2,1)S(1)}, bf16[2,2,160,128]{3,2,1,0:T(8,128)(2,1)S(1)}, u32[]{:S(2)}, u32[]{:S(2)}) %collective-permute-start.13) | collective-permute-done | bytes 163872 | tf_op jit(solution)/shard_map/ppermute | solution.py:57
  45.7 1.4 %collective-permute-start.14 = (bf16[2,2,160,128]{3,2,1,0:T(8,128)(2,1)S(1)}, bf16[2,2,160,128]{3,2,1,0:T(8,128)(2,1)S(1)}, u32[]{:S(2)}, u32[]{:S(2)}) collective-permute-start(bf16[2,2,160,128]{3,2,1,0:T(8,128)(2,1)S(1)} %collective-permute-done.13.own), channel_id=1, source_target_pairs={{0,2},{2,0},{1,3},{3,1},{4,6},{6,4},{5,7},{7,5},{8,10},{10,8},{9,1... | collective-permute-start | bytes 491528 | tf_op jit(solution)/shard_map/ppermute | solution.py:44
  47.1 2.4 %collective-permute-start.17 = (bf16[2,2,160,128]{3,2,1,0:T(8,128)(2,1)S(1)}, bf16[2,2,160,128]{3,2,1,0:T(8,128)(2,1)S(1)}, u32[]{:S(2)}, u32[]{:S(2)}) collective-permute-start(bf16[2,2,160,128]{3,2,1,0:T(8,128)(2,1)S(1)} %fold.12), channel_id=1, source_target_pairs={{0,16},{1,21},{2,18},{3,23},{4,20},{5,17},{6,22},{7,19},{8,24},{9,... | collective-permute-start | bytes 491528 | tf_op jit(solution)/shard_map/ppermute | solution.py:57
  49.5 0.7 %collective-permute-start.19 = (bf16[2,2,160,128]{3,2,1,0:T(8,128)(2,1)S(1)}, bf16[2,2,160,128]{3,2,1,0:T(8,128)(2,1)S(1)}, u32[]{:S(2)}, u32[]{:S(2)}) collective-permute-start(bf16[2,2,160,128]{3,2,1,0:T(8,128)(2,1)S(1)} %collective-permute-done.18.own), channel_id=1, source_target_pairs={{0,2},{2,0},{1,3},{3,1},{4,6},{6,4},{5,7},{7,5},{8,10},{10,8},{9,1... | collective-permute-start | bytes 491528 | tf_op jit(solution)/shard_map/ppermute | solution.py:44
  51.0 2.1 %collective-permute-done.14.peer = bf16[2,2,160,128]{3,2,1,0:T(8,128)(2,1)S(1)} collective-permute-done((bf16[2,2,160,128]{3,2,1,0:T(8,128)(2,1)S(1)}, bf16[2,2,160,128]{3,2,1,0:T(8,128)(2,1)S(1)}, u32[]{:S(2)}, u32[]{:S(2)}) %collective-permute-start.14) | collective-permute-done | bytes 163872 | tf_op jit(solution)/shard_map/ppermute | solution.py:44
  53.1 2.7 %collective-permute-done.17.refs_2_ = bf16[2,2,160,128]{3,2,1,0:T(8,128)(2,1)S(1)} collective-permute-done((bf16[2,2,160,128]{3,2,1,0:T(8,128)(2,1)S(1)}, bf16[2,2,160,128]{3,2,1,0:T(8,128)(2,1)S(1)}, u32[]{:S(2)}, u32[]{:S(2)}) %collective-permute-start.17) | collective-permute-done | bytes 163872 | tf_op jit(solution)/shard_map/ppermute | solution.py:57
  56.2 1.6 %collective-permute-done.23.got = bf16[4,2,160,128]{3,2,1,0:T(8,128)(2,1)S(1)} collective-permute-done((bf16[4,2,160,128]{3,2,1,0:T(8,128)(2,1)S(1)}, bf16[4,2,160,128]{3,2,1,0:T(8,128)(2,1)S(1)}, u32[]{:S(2)}, u32[]{:S(2)}) %collective-permute-start.23) | collective-permute-done | bytes 327712 | tf_op jit(solution)/shard_map/ppermute | solution.py:44
  57.8 1.8 %place.1 = (bf16[160,16,128]{2,1,0:T(8,128)(2,1)}, bf16[640,512]{1,0:T(8,128)(2,1)}) custom-call(s32[16]{0:T(128)S(1)} %copy-done.4, bf16[4,2,160,128]{3,2,1,0:T(8,128)(2,1)S(1)} %get-tuple-element.66.keep, bf16[4,2,160,128]{3,2,1,0:T(8,128)(2,1)S(1)} %collective-permute-done.23.got, bf16[640,256]{1,0:T(8,128)(2,1)S(1)} %get-tuple-element.68.spec_mine, ...), custom_call_target="tpu_custom_call" | custom-call | bytes 2621504 | tf_op jit(solution)/shard_map/place/pallas_call | solution.py:130
  (56 shorter events, 8.8 us)
Async XLA Ops:
  4.6 1.5 %collective-permute-start = (bf16[2,2,160,128]{3,2,1,0:T(8,128)(2,1)S(1)}, bf16[2,2,160,128]{3,2,1,0:T(8,128)(2,1)S(1)}, u32[]{:S(2)}, u32[]{:S(2)}) collective-permute-start(bf16[2,2,160,128]{3,2,1,0:T(8,128)(2,1)S(1)} %get-tuple-element.38), channel_id=1, source_target_pairs={{0,1},{1,0},{2,3},{3,2},{4,5},{5,4},{6,7},{7,6},{8,9},{9,8},{10,11... | collective-permute-start | bytes 491528 | tf_op jit(solution)/shard_map/ppermute | solution.py:44
  5.1 1.4 %collective-permute-start.3 = (bf16[2,2,160,128]{3,2,1,0:T(8,128)(2,1)S(1)}, bf16[2,2,160,128]{3,2,1,0:T(8,128)(2,1)S(1)}, u32[]{:S(2)}, u32[]{:S(2)}) collective-permute-start(bf16[2,2,160,128]{3,2,1,0:T(8,128)(2,1)S(1)} %get-tuple-element.41), channel_id=1, source_target_pairs={{0,1},{1,0},{2,3},{3,2},{4,5},{5,4},{6,7},{7,6},{8,9},{9,8},{10,11... | collective-permute-start | bytes 491528 | tf_op jit(solution)/shard_map/ppermute | solution.py:44
  6.5 22.3 %collective-permute-start.10 = (bf16[2,1,640,1280]{3,2,1,0:T(8,128)(2,1)}, bf16[2,1,640,1280]{3,2,1,0:T(8,128)(2,1)S(1)}, u32[]{:S(2)}, u32[]{:S(2)}) collective-permute-start(bf16[2,1,640,1280]{3,2,1,0:T(8,128)(2,1)} %tables_mine.1), channel_id=1, source_target_pairs={{0,1},{1,0},{2,3},{3,2},{4,5},{5,4},{6,7},{7,6},{8,9},{9,8},{10,11... | collective-permute-start | bytes 9830408 | tf_op jit(solution)/shard_map/ppermute | solution.py:44
  6.8 10.9 %collective-permute-start.1 = (bf16[2,2,160,128]{3,2,1,0:T(8,128)(2,1)S(1)}, bf16[2,2,160,128]{3,2,1,0:T(8,128)(2,1)S(1)}, u32[]{:S(2)}, u32[]{:S(2)}) collective-permute-start(bf16[2,2,160,128]{3,2,1,0:T(8,128)(2,1)S(1)} %get-tuple-element.39), channel_id=1, source_target_pairs={{0,28},{1,25},{2,30},{3,27},{4,24},{5,29},{6,26},{7,31},{8,20},{9,... | collective-permute-start | bytes 491528 | tf_op jit(solution)/shard_map/ppermute | solution.py:57
  12.7 7.2 %collective-permute-start.4 = (bf16[2,2,160,128]{3,2,1,0:T(8,128)(2,1)S(1)}, bf16[2,2,160,128]{3,2,1,0:T(8,128)(2,1)S(1)}, u32[]{:S(2)}, u32[]{:S(2)}) collective-permute-start(bf16[2,2,160,128]{3,2,1,0:T(8,128)(2,1)S(1)} %get-tuple-element.42.own), channel_id=1, source_target_pairs={{0,2},{2,0},{1,3},{3,1},{4,6},{6,4},{5,7},{7,5},{8,10},{10,8},{9,1... | collective-permute-start | bytes 491528 | tf_op jit(solution)/shard_map/ppermute | solution.py:44
  14.2 8.9 %collective-permute-start.6 = (bf16[2,2,160,128]{3,2,1,0:T(8,128)(2,1)S(1)}, bf16[2,2,160,128]{3,2,1,0:T(8,128)(2,1)S(1)}, u32[]{:S(2)}, u32[]{:S(2)}) collective-permute-start(bf16[2,2,160,128]{3,2,1,0:T(8,128)(2,1)S(1)} %get-tuple-element.44), channel_id=1, source_target_pairs={{0,4},{1,13},{2,6},{3,15},{4,0},{5,9},{6,2},{7,11},{8,12},{9,5},{1... | collective-permute-start | bytes 491528 | tf_op jit(solution)/shard_map/ppermute | solution.py:57
  14.8 8.9 %collective-permute-start.8 = (bf16[2,2,160,128]{3,2,1,0:T(8,128)(2,1)S(1)}, bf16[2,2,160,128]{3,2,1,0:T(8,128)(2,1)S(1)}, u32[]{:S(2)}, u32[]{:S(2)}) collective-permute-start(bf16[2,2,160,128]{3,2,1,0:T(8,128)(2,1)S(1)} %get-tuple-element.45.own), channel_id=1, source_target_pairs={{0,2},{2,0},{1,3},{3,1},{4,6},{6,4},{5,7},{7,5},{8,10},{10,8},{9,1... | collective-permute-start | bytes 491528 | tf_op jit(solution)/shard_map/ppermute | solution.py:44
  17.7 7.5 %collective-permute-start.2 = (bf16[2,2,160,128]{3,2,1,0:T(8,128)(2,1)S(1)}, bf16[2,2,160,128]{3,2,1,0:T(8,128)(2,1)S(1)}, u32[]{:S(2)}, u32[]{:S(2)}) collective-permute-start(bf16[2,2,160,128]{3,2,1,0:T(8,128)(2,1)S(1)} %collective-permute-done.1.own), channel_id=1, source_target_pairs={{0,2},{2,0},{1,3},{3,1},{4,6},{6,4},{5,7},{7,5},{8,10},{10,8},{9,1... | collective-permute-start | bytes 491528 | tf_op jit(solution)/shard_map/ppermute | solution.py:44
  19.9 8.8 %collective-permute-start.5 = (bf16[2,2,160,128]{3,2,1,0:T(8,128)(2,1)S(1)}, bf16[2,2,160,128]{3,2,1,0:T(8,128)(2,1)S(1)}, u32[]{:S(2)}, u32[]{:S(2)}) collective-permute-start(bf16[2,2,160,128]{3,2,1,0:T(8,128)(2,1)S(1)} %fold.8), channel_id=1, source_target_pairs={{0,16},{1,21},{2,18},{3,23},{4,20},{5,17},{6,22},{7,19},{8,24},{9,... | collective-permute-start | bytes 491528 | tf_op jit(solution)/shard_map/ppermute | solution.py:57
  23.1 5.6 %collective-permute-start.7 = (bf16[2,2,160,128]{3,2,1,0:T(8,128)(2,1)S(1)}, bf16[2,2,160,128]{3,2,1,0:T(8,128)(2,1)S(1)}, u32[]{:S(2)}, u32[]{:S(2)}) collective-permute-start(bf16[2,2,160,128]{3,2,1,0:T(8,128)(2,1)S(1)} %collective-permute-done.6.own), channel_id=1, source_target_pairs={{0,2},{2,0},{1,3},{3,1},{4,6},{6,4},{5,7},{7,5},{8,10},{10,8},{9,1... | collective-permute-start | bytes 491528 | tf_op jit(solution)/shard_map/ppermute | solution.py:44
  23.8 5.1 %collective-permute-start.9 = (bf16[2,2,160,128]{3,2,1,0:T(8,128)(2,1)S(1)}, bf16[2,2,160,128]{3,2,1,0:T(8,128)(2,1)S(1)}, u32[]{:S(2)}, u32[]{:S(2)}) collective-permute-start(bf16[2,2,160,128]{3,2,1,0:T(8,128)(2,1)S(1)} %fold.11.refs_4_), channel_id=1, source_target_pairs={{1,9},{3,11},{5,13},{7,15},{9,1},{11,3},{13,5},{15,7},{17,25},{19,... | collective-permute-start | bytes 491528 | tf_op jit(solution)/shard_map/ppermute | solution.py:57
  29.0 1.8 %collective-permute-start.11 = (bf16[4,2,160,128]{3,2,1,0:T(8,128)(2,1)S(1)}, bf16[4,2,160,128]{3,2,1,0:T(8,128)(2,1)S(1)}, u32[]{:S(2)}, u32[]{:S(2)}) collective-permute-start(bf16[4,2,160,128]{3,2,1,0:T(8,128)(2,1)S(1)} %get-tuple-element.49), channel_id=1, source_target_pairs={{0,1},{1,0},{2,3},{3,2},{4,5},{5,4},{6,7},{7,6},{8,9},{9,8},{10,11... | collective-permute-start | bytes 983048 | tf_op jit(solution)/shard_map/ppermute | solution.py:44
  34.3 1.5 %collective-permute-start.12 = (bf16[2,2,160,128]{3,2,1,0:T(8,128)(2,1)S(1)}, bf16[2,2,160,128]{3,2,1,0:T(8,128)(2,1)S(1)}, u32[]{:S(2)}, u32[]{:S(2)}) collective-permute-start(bf16[2,2,160,128]{3,2,1,0:T(8,128)(2,1)S(1)} %get-tuple-element.55), channel_id=1, source_target_pairs={{0,1},{1,0},{2,3},{3,2},{4,5},{5,4},{6,7},{7,6},{8,9},{9,8},{10,11... | collective-permute-start | bytes 491528 | tf_op jit(solution)/shard_map/ppermute | solution.py:44
  34.8 4.2 %collective-permute-start.15 = (bf16[2,2,160,128]{3,2,1,0:T(8,128)(2,1)S(1)}, bf16[2,2,160,128]{3,2,1,0:T(8,128)(2,1)S(1)}, u32[]{:S(2)}, u32[]{:S(2)}) collective-permute-start(bf16[2,2,160,128]{3,2,1,0:T(8,128)(2,1)S(1)} %get-tuple-element.58), channel_id=1, source_target_pairs={{0,1},{1,0},{2,3},{3,2},{4,5},{5,4},{6,7},{7,6},{8,9},{9,8},{10,11... | collective-permute-start | bytes 491528 | tf_op jit(solution)/shard_map/ppermute | solution.py:44
  35.8 9.8 %collective-permute-start.13 = (bf16[2,2,160,128]{3,2,1,0:T(8,128)(2,1)S(1)}, bf16[2,2,160,128]{3,2,1,0:T(8,128)(2,1)S(1)}, u32[]{:S(2)}, u32[]{:S(2)}) collective-permute-start(bf16[2,2,160,128]{3,2,1,0:T(8,128)(2,1)S(1)} %get-tuple-element.56), channel_id=1, source_target_pairs={{0,28},{1,25},{2,30},{3,27},{4,24},{5,29},{6,26},{7,31},{8,20},{9,... | collective-permute-start | bytes 491528 | tf_op jit(solution)/shard_map/ppermute | solution.py:57
  39.0 8.1 %collective-permute-start.16 = (bf16[2,2,160,128]{3,2,1,0:T(8,128)(2,1)S(1)}, bf16[2,2,160,128]{3,2,1,0:T(8,128)(2,1)S(1)}, u32[]{:S(2)}, u32[]{:S(2)}) collective-permute-start(bf16[2,2,160,128]{3,2,1,0:T(8,128)(2,1)S(1)} %get-tuple-element.59.own), channel_id=1, source_target_pairs={{0,2},{2,0},{1,3},{3,1},{4,6},{6,4},{5,7},{7,5},{8,10},{10,8},{9,1... | collective-permute-start | bytes 491528 | tf_op jit(solution)/shard_map/ppermute | solution.py:44
  39.6 16.2 %collective-permute-start.22 = (bf16[640,256]{1,0:T(8,128)(2,1)S(1)}, bf16[640,256]{1,0:T(8,128)(2,1)S(1)}, u32[]{:S(2)}, u32[]{:S(2)}) collective-permute-start(bf16[640,256]{1,0:T(8,128)(2,1)S(1)} %get-tuple-element.64), channel_id=1, source_target_pairs={{0,1},{1,0},{2,3},{3,2},{4,5},{5,4},{6,7},{7,6},{8,9},{9,8},{10,11... | collective-permute-start | bytes 983048 | tf_op jit(solution)/shard_map/ppermute | solution.py:44
  39.6 9.8 %collective-permute-start.18 = (bf16[2,2,160,128]{3,2,1,0:T(8,128)(2,1)S(1)}, bf16[2,2,160,128]{3,2,1,0:T(8,128)(2,1)S(1)}, u32[]{:S(2)}, u32[]{:S(2)}) collective-permute-start(bf16[2,2,160,128]{3,2,1,0:T(8,128)(2,1)S(1)} %get-tuple-element.61), channel_id=1, source_target_pairs={{0,4},{1,13},{2,6},{3,15},{4,0},{5,9},{6,2},{7,11},{8,12},{9,5},{1... | collective-permute-start | bytes 491528 | tf_op jit(solution)/shard_map/ppermute | solution.py:57
  41.4 8.8 %collective-permute-start.20 = (bf16[2,2,160,128]{3,2,1,0:T(8,128)(2,1)S(1)}, bf16[2,2,160,128]{3,2,1,0:T(8,128)(2,1)S(1)}, u32[]{:S(2)}, u32[]{:S(2)}) collective-permute-start(bf16[2,2,160,128]{3,2,1,0:T(8,128)(2,1)S(1)} %get-tuple-element.62.own), channel_id=1, source_target_pairs={{0,2},{2,0},{1,3},{3,1},{4,6},{6,4},{5,7},{7,5},{8,10},{10,8},{9,1... | collective-permute-start | bytes 491528 | tf_op jit(solution)/shard_map/ppermute | solution.py:44
  45.7 7.4 %collective-permute-start.14 = (bf16[2,2,160,128]{3,2,1,0:T(8,128)(2,1)S(1)}, bf16[2,2,160,128]{3,2,1,0:T(8,128)(2,1)S(1)}, u32[]{:S(2)}, u32[]{:S(2)}) collective-permute-start(bf16[2,2,160,128]{3,2,1,0:T(8,128)(2,1)S(1)} %collective-permute-done.13.own), channel_id=1, source_target_pairs={{0,2},{2,0},{1,3},{3,1},{4,6},{6,4},{5,7},{7,5},{8,10},{10,8},{9,1... | collective-permute-start | bytes 491528 | tf_op jit(solution)/shard_map/ppermute | solution.py:44
  47.1 8.7 %collective-permute-start.17 = (bf16[2,2,160,128]{3,2,1,0:T(8,128)(2,1)S(1)}, bf16[2,2,160,128]{3,2,1,0:T(8,128)(2,1)S(1)}, u32[]{:S(2)}, u32[]{:S(2)}) collective-permute-start(bf16[2,2,160,128]{3,2,1,0:T(8,128)(2,1)S(1)} %fold.12), channel_id=1, source_target_pairs={{0,16},{1,21},{2,18},{3,23},{4,20},{5,17},{6,22},{7,19},{8,24},{9,... | collective-permute-start | bytes 491528 | tf_op jit(solution)/shard_map/ppermute | solution.py:57
  49.5 6.4 %collective-permute-start.19 = (bf16[2,2,160,128]{3,2,1,0:T(8,128)(2,1)S(1)}, bf16[2,2,160,128]{3,2,1,0:T(8,128)(2,1)S(1)}, u32[]{:S(2)}, u32[]{:S(2)}) collective-permute-start(bf16[2,2,160,128]{3,2,1,0:T(8,128)(2,1)S(1)} %collective-permute-done.18.own), channel_id=1, source_target_pairs={{0,2},{2,0},{1,3},{3,1},{4,6},{6,4},{5,7},{7,5},{8,10},{10,8},{9,1... | collective-permute-start | bytes 491528 | tf_op jit(solution)/shard_map/ppermute | solution.py:44
  50.3 5.7 %collective-permute-start.21 = (bf16[2,2,160,128]{3,2,1,0:T(8,128)(2,1)S(1)}, bf16[2,2,160,128]{3,2,1,0:T(8,128)(2,1)S(1)}, u32[]{:S(2)}, u32[]{:S(2)}) collective-permute-start(bf16[2,2,160,128]{3,2,1,0:T(8,128)(2,1)S(1)} %fold.15.refs_4_), channel_id=1, source_target_pairs={{1,9},{3,11},{5,13},{7,15},{9,1},{11,3},{13,5},{15,7},{17,25},{19,... | collective-permute-start | bytes 491528 | tf_op jit(solution)/shard_map/ppermute | solution.py:57
  56.1 1.7 %collective-permute-start.23 = (bf16[4,2,160,128]{3,2,1,0:T(8,128)(2,1)S(1)}, bf16[4,2,160,128]{3,2,1,0:T(8,128)(2,1)S(1)}, u32[]{:S(2)}, u32[]{:S(2)}) collective-permute-start(bf16[4,2,160,128]{3,2,1,0:T(8,128)(2,1)S(1)} %get-tuple-element.67), channel_id=1, source_target_pairs={{0,1},{1,0},{2,3},{3,2},{4,5},{5,4},{6,7},{7,6},{8,9},{9,8},{10,11... | collective-permute-start | bytes 983048 | tf_op jit(solution)/shard_map/ppermute | solution.py:44
  (7 other events, 111.4 us)
